TPU v7x, 512 devices: a whole 4x8x8 slice. The times are simulated.
512 devices in a mesh: aa: 32 (over x, y_lo, core), ba: 16 (over z, y_hi).
Axes of the slice: x: 4, y: 8 (y_hi: 2, y_lo: 4; y = y_hi * 4 + y_lo), z: 8, core: 2. Of those that a mesh axis runs over, the one named last changes fastest.
Arguments:
- field: float32 [32, 2048, 2048], P('aa', None, 'ba'), may hold values from -6 to 6
- gains: float32 [2, 2, 2], replicated, may hold values from 0.25 to 4
Outputs:
- coefficients: float32 [32, 2048, 2048], P(None, 'aa', 'ba')
- rebuilt: float32 [32, 2048, 2048], P('aa', None, 'ba')
All inputs are finite; a program needn't handle non-finite values.
Results may differ from a plain program's by a relative error of at most 0.00002.
Values sent between devices are 32-bit elements; how exact they have to be, the bound alone decides.
No kernel may reach another device: no remote copies, remote signals or barrier semaphores. Data moves between devices by JAX's collectives and lax.ppermute only.
A program may use at most 64 MiB of HBM per device.

v0:
```python
import jax
import jax.numpy as jnp
from jax import lax
from jax.sharding import PartitionSpec as P

predict_first = -1.586134342059924
update_first = -0.052980118572961
predict_second = 0.882911075530934
update_second = 0.443506852043971
balance = 1.230174104914001


def take_range(values, begin, finish, dimension):
    return lax.slice_in_dim(values, begin, finish, 1, dimension)


def mirror(values, dimension):
    extent = values.shape[dimension]
    lower_rim = jnp.flip(take_range(values, 1, 5, dimension), dimension)
    upper_rim = jnp.flip(take_range(values, extent - 5, extent - 1, dimension), dimension)
    return jnp.concatenate([lower_rim, values, upper_rim], dimension)


def split_parity(extended, dimension):
    length = extended.shape[dimension]
    even_part = lax.slice_in_dim(extended, 0, length, 2, dimension)
    odd_part = lax.slice_in_dim(extended, 1, length, 2, dimension)
    return (even_part, odd_part)


def alternate(low_band, high_band, dimension):
    joined = jnp.stack([low_band, high_band], axis=dimension + 1)
    new_shape = list(low_band.shape)
    new_shape[dimension] = 2 * new_shape[dimension]
    return joined.reshape(new_shape)


def analyse(extended, dimension):
    even_part, odd_part = split_parity(extended, dimension)
    length = even_part.shape[dimension]
    lift_one = take_range(odd_part, 0, length - 1, dimension) + predict_first * (
        take_range(even_part, 0, length - 1, dimension)
        + take_range(even_part, 1, length, dimension)
    )
    lift_two = take_range(even_part, 1, length - 1, dimension) + update_first * (
        take_range(lift_one, 0, length - 2, dimension)
        + take_range(lift_one, 1, length - 1, dimension)
    )
    lift_three = take_range(lift_one, 1, length - 2, dimension) + predict_second * (
        take_range(lift_two, 0, length - 3, dimension)
        + take_range(lift_two, 1, length - 2, dimension)
    )
    lift_four = take_range(lift_two, 1, length - 3, dimension) + update_second * (
        take_range(lift_three, 0, length - 4, dimension)
        + take_range(lift_three, 1, length - 3, dimension)
    )
    high_band = take_range(lift_three, 1, length - 3, dimension)
    return alternate(lift_four / balance, high_band * balance, dimension)


def synthesise(extended, dimension):
    even_part, odd_part = split_parity(extended, dimension)
    length = even_part.shape[dimension]
    low_band = even_part * balance
    high_band = odd_part / balance
    lift_one = take_range(low_band, 1, length, dimension) - update_second * (
        take_range(high_band, 0, length - 1, dimension)
        + take_range(high_band, 1, length, dimension)
    )
    lift_two = take_range(high_band, 1, length - 1, dimension) - predict_second * (
        take_range(lift_one, 0, length - 2, dimension)
        + take_range(lift_one, 1, length - 1, dimension)
    )
    lift_three = take_range(lift_one, 1, length - 2, dimension) - update_first * (
        take_range(lift_two, 0, length - 3, dimension)
        + take_range(lift_two, 1, length - 2, dimension)
    )
    lift_four = take_range(lift_two, 1, length - 3, dimension) - predict_first * (
        take_range(lift_three, 0, length - 4, dimension)
        + take_range(lift_three, 1, length - 3, dimension)
    )
    return alternate(take_range(lift_three, 0, length - 4, dimension), lift_four, dimension)


def apply_gains(coefficients, gains):
    depth_cells, column_cells, row_cells = coefficients.shape
    parity = jnp.arange(row_cells) % 2
    gain_table = jnp.where(parity[None, None, :] == 0, gains[:, :, 0:1], gains[:, :, 1:2])
    grouped = coefficients.reshape(depth_cells // 2, 2, column_cells // 2, 2, row_cells)
    return (grouped * gain_table[None, :, None, :, :]).reshape(coefficients.shape)


def along_rows(values, lifting):
    by_rows = lax.all_to_all(values, "ba", split_axis=1, concat_axis=2, tiled=True)
    by_rows = lifting(mirror(by_rows, 2), 2)
    return lax.all_to_all(by_rows, "ba", split_axis=2, concat_axis=1, tiled=True)


def per_device(field, gains):
    sectioned = along_rows(field, analyse)
    sectioned = analyse(mirror(sectioned, 1), 1)
    by_depth = lax.all_to_all(sectioned, "aa", split_axis=1, concat_axis=0, tiled=True)
    coefficients = analyse(mirror(by_depth, 0), 0)
    rebuilt = synthesise(mirror(apply_gains(coefficients, gains), 0), 0)
    rebuilt = lax.all_to_all(rebuilt, "aa", split_axis=0, concat_axis=1, tiled=True)
    rebuilt = synthesise(mirror(rebuilt, 1), 1)
    rebuilt = along_rows(rebuilt, synthesise)
    return (coefficients, rebuilt)


def solution(mesh):
    return jax.shard_map(
        per_device,
        mesh=mesh,
        in_specs=(P("aa", None, "ba"), P()),
        out_specs=(P(None, "aa", "ba"), P("aa", None, "ba")),
        check_vma=False,
    )
```

profile of v0, /device:TPU:184, one launch (start us, length us, event | category | flops | bytes accessed | tf_op | source)
XLA Modules:
  0.0 266.1 jit_solution(1337783043403245512)
XLA Ops:
  0.6 39.7 %all_to_all.99 = f32[1,2048,128]{2,0,1:T(1,128)S(1)} all-to-all(f32[1,2048,128]{2,0,1:T(1,128)} %bitcast.87), channel_id=1, replica_groups=mesh['aa'=32,'ba'=16] {'ba'}, dimensions={1} | all-to-all | bytes 2097152 | tf_op jit(solution)/shard_map/all_to_all | solution.py:94
  40.3 0.3 copy.47
  40.7 1.3 concatenate.19
  42.0 0.7 slice.308
  42.7 0.7 slice.310
  43.8 0.2 fusion.54
  44.0 0.8 copy.48
  44.8 35.4 %all_to_all.100 = f32[1,128,2048]{1,0,2:T(1,128)S(1)} all-to-all(f32[1,128,2048]{1,0,2:T(1,128)S(1)} %bitcast.79), channel_id=1, replica_groups=mesh['aa'=32,'ba'=16] {'ba'}, dimensions={2} | all-to-all | bytes 2097152 | tf_op jit(solution)/shard_map/all_to_all | solution.py:96
  80.2 0.3 copy.50
  80.6 1.3 concatenate.20
  81.9 0.7 slice.324
  82.6 0.7 slice.326
  84.0 1.8 copy.51
  85.7 14.1 %all-to-all-start.2 = ((f32[1,2048,128]{2,0,1:T(1,128)}), f32[1,2048,128]{2,0,1:T(1,128)S(1)}, u32[]{:S(2)}, u32[]{:S(2)}) async-start(f32[1,2048,128]{2,0,1:T(1,128)} %bitcast.14), calls=%async_computation.2 | async-start | bytes 2097152 | tf_op jit(solution)/shard_map/all_to_all | solution.py:102
  100.1 23.6 %all-to-all-done.2 = f32[1,2048,128]{2,0,1:T(1,128)S(1)} async-done(((f32[1,2048,128]{2,0,1:T(1,128)}), f32[1,2048,128]{2,0,1:T(1,128)S(1)}, u32[]{:S(2)}, u32[]{:S(2)}) %all-to-all-start.2) | async-done | bytes 1048608 | tf_op jit(solution)/shard_map/all_to_all | solution.py:102
  124.3 1.0 slice_multiply_fusion.4
  125.3 0.7 maximum_multiply_fusion
  126.9 31.5 %all_to_all.101 = f32[32,64,128]{2,1,0:T(8,128)S(1)} all-to-all(f32[32,64,128]{2,1,0:T(8,128)S(1)} %bitcast.81), channel_id=1, replica_groups=mesh['aa'=32,'ba'=16] {'aa'}, dimensions={0} | all-to-all | bytes 2097152 | tf_op jit(solution)/shard_map/all_to_all | solution.py:105
  158.5 1.3 concatenate.23
  159.8 0.7 slice.378
  160.5 0.7 slice.376
  161.8 0.9 pad_maximum_fusion.6
  162.8 39.7 %all_to_all.102 = f32[1,2048,128]{2,0,1:T(1,128)S(1)} all-to-all(f32[1,2048,128]{2,0,1:T(1,128)S(1)} %bitcast.78), channel_id=1, replica_groups=mesh['aa'=32,'ba'=16] {'ba'}, dimensions={1} | all-to-all | bytes 2097152 | tf_op jit(solution)/shard_map/all_to_all | solution.py:94
  202.5 0.3 copy.57
  202.9 1.3 concatenate.24
  204.2 0.7 slice.394
  204.9 0.7 slice.392
  206.3 1.8 copy.58
  208.1 10.3 %all-to-all-start.5 = ((f32[1,128,2048]{1,0,2:T(1,128)}), f32[1,128,2048]{1,0,2:T(1,128)S(1)}, u32[]{:S(2)}, u32[]{:S(2)}) async-start(f32[1,128,2048]{1,0,2:T(1,128)} %bitcast.40), calls=%async_computation.5 | async-start | bytes 2097152 | tf_op jit(solution)/shard_map/all_to_all | solution.py:96
  218.5 1.1 copy.53
  219.6 45.2 %all-to-all-done.5 = f32[1,128,2048]{1,0,2:T(1,128)S(1)} async-done(((f32[1,128,2048]{1,0,2:T(1,128)}), f32[1,128,2048]{1,0,2:T(1,128)S(1)}, u32[]{:S(2)}, u32[]{:S(2)}) %all-to-all-start.5) | async-done | bytes 1048608 | tf_op jit(solution)/shard_map/all_to_all | solution.py:96
  264.8 1.3 copy.60
  (60 shorter events, 4.2 us)
Async XLA Ops:
  85.7 14.1 %copy-start.1 = (f32[2,2,2]{2,1,0:T(2,128)S(1)}, f32[2,2,2]{2,1,0:T(2,128)}, u32[]{:S(2)}) copy-start(f32[2,2,2]{2,1,0:T(2,128)} %param.3) | copy-start | bytes 100
  85.7 38.0 %all-to-all-start.2 = ((f32[1,2048,128]{2,0,1:T(1,128)}), f32[1,2048,128]{2,0,1:T(1,128)S(1)}, u32[]{:S(2)}, u32[]{:S(2)}) async-start(f32[1,2048,128]{2,0,1:T(1,128)} %bitcast.14), calls=%async_computation.2 | async-start | bytes 2097152 | tf_op jit(solution)/shard_map/all_to_all | solution.py:102
  208.1 10.3 %copy-start = (f32[16,1,64,128]{3,2,0,1:T(8,128)S(1)}, f32[16,1,64,128]{3,2,0,1:T(8,128)}, u32[]{:S(2)}) copy-start(f32[16,1,64,128]{3,2,0,1:T(8,128)} %get-tuple-element.21) | copy-start | bytes 1572868
  208.1 56.7 %all-to-all-start.5 = ((f32[1,128,2048]{1,0,2:T(1,128)}), f32[1,128,2048]{1,0,2:T(1,128)S(1)}, u32[]{:S(2)}, u32[]{:S(2)}) async-start(f32[1,128,2048]{1,0,2:T(1,128)} %bitcast.40), calls=%async_computation.5 | async-start | bytes 2097152 | tf_op jit(solution)/shard_map/all_to_all | solution.py:96
where the time goes:
time: 267 us; the launch traced here: 266 us
  blocking collectives  146 us (55%)
  waiting for transfers between devices  68.8 us (26%)
  starting transfers between devices  24.4 us (9%)
  local copies, waits for them, and re-layouts  19.3 us (7%)
  other arithmetic  6.26 us (2%)
    all_to_all x2, blocking collectives, along_rows(): lax.all_to_all(values, 'ba', split_axis=1, concat_axis=2, tiled=True)  79.4 us
    all_to_all x1, waiting for transfers between devices, along_rows(): lax.all_to_all(by_rows, 'ba', split_axis=2, concat_axis=1, tiled=True)  45.2 us
    all_to_all x1, blocking collectives, along_rows(): lax.all_to_all(by_rows, 'ba', split_axis=2, concat_axis=1, tiled=True)  35.4 us
    all_to_all x1, blocking collectives, per_device(): lax.all_to_all(rebuilt, 'aa', split_axis=0, concat_axis=1, tiled=True)  31.5 us
    all_to_all x1, waiting for transfers between devices, per_device(): lax.all_to_all(sectioned, 'aa', split_axis=1, concat_axis=0, tiled=True)  23.6 us
    all_to_all x1, starting transfers between devices, per_device(): lax.all_to_all(sectioned, 'aa', split_axis=1, concat_axis=0, tiled=True)  14.1 us
    all_to_all x1, starting transfers between devices, along_rows(): lax.all_to_all(by_rows, 'ba', split_axis=2, concat_axis=1, tiled=True)  10.3 us
    another operation x5, local copies, waits for them, and re-layouts, alternate(): joined = jnp.stack([low_band, high_band], axis=dimension + 1)  5.56 us
  transfers between devices with their start and end apart: 2, of which 2 were waited for; matrix products, arithmetic and copies ran while one was open for 1% of the time, Pallas kernels for 0%

commit v1 on v0

v1 whole, which is shorter than its diff:
```python
import functools

import jax
import jax.numpy as jnp
import numpy as np
from jax import lax
from jax.experimental import pallas as pl
from jax.experimental.pallas import tpu as pltpu
from jax.sharding import PartitionSpec as P

PREDICT_FIRST = -1.586134342059924
UPDATE_FIRST = -0.052980118572961
PREDICT_SECOND = 0.882911075530934
UPDATE_SECOND = 0.443506852043971
BALANCE = 1.230174104914001

X = 128
HALF = X // 2
HALO = 8
ROWS = 8
MARGIN = 16
VMEM_LIMIT = 48 * 1024 * 1024


def edge_matrix():
    unit = np.eye(X)
    s, d = unit[0::2], unit[1::2]
    d1 = [d[n] + PREDICT_FIRST * (s[n] + s[n + 1]) for n in range(HALF - 1)]
    s1 = [None] + [s[n] + UPDATE_FIRST * (d1[n - 1] + d1[n]) for n in range(1, HALF - 1)]
    out = np.zeros((HALO, X))
    out[0] = s[0]
    out[1] = d1[0]
    out[2] = s1[1]
    out[3] = d1[1] + PREDICT_SECOND * (s1[1] + s1[2])
    last = HALF - 1
    out[4] = d[last] + PREDICT_FIRST * s[last]
    out[5] = s[last] + UPDATE_FIRST * d1[last - 1]
    out[6] = d1[last - 1] + PREDICT_SECOND * s1[last - 1]
    return out


def analysis_matrix(left_end, right_end):
    unit = np.eye(2 * X)
    cell, halo = unit[:X], unit[X : X + HALO]
    n_all = HALF
    s = {n: cell[2 * n] for n in range(n_all)}
    d = {n: cell[2 * n + 1] for n in range(n_all)}
    s[n_all] = s[n_all - 1] if right_end else halo[0]
    d1 = {n: d[n] + PREDICT_FIRST * (s[n] + s[n + 1]) for n in range(n_all)}
    d1[n_all] = d1[n_all - 2] if right_end else halo[1]
    d1[-1] = d1[0] if left_end else halo[4] + PREDICT_FIRST * s[0]
    s1 = {n: s[n] + UPDATE_FIRST * (d1[n - 1] + d1[n]) for n in range(n_all + 1)}
    s1[n_all + 1] = s1[n_all - 2] if right_end else halo[2]
    s1[-1] = s1[1] if left_end else halo[5] + UPDATE_FIRST * d1[-1]
    d2 = {n: d1[n] + PREDICT_SECOND * (s1[n] + s1[n + 1]) for n in range(-1, n_all + 1)}
    d2[n_all + 1] = d2[n_all - 3] if right_end else halo[3]
    d2[-2] = d2[1] if left_end else halo[6] + PREDICT_SECOND * s1[-1]
    s2 = {n: s1[n] + UPDATE_SECOND * (d2[n - 1] + d2[n]) for n in range(-1, n_all + 2)}
    out = np.zeros((2 * X, 2 * X))
    for n in range(n_all):
        out[:, 2 * n] = s2[n] / BALANCE
        out[:, 2 * n + 1] = d2[n] * BALANCE
    beyond = [
        s2[n_all] / BALANCE, d2[n_all] * BALANCE, s2[n_all + 1] / BALANCE, d2[n_all + 1] * BALANCE,
        d2[-1] * BALANCE, s2[-1] / BALANCE, d2[-2] * BALANCE,
    ]
    for k, row in enumerate(beyond):
        out[:, X + k] = row
    return out


def synthesis_matrix():
    unit = np.eye(2 * X)
    n_all = HALF
    place = {k: k for k in range(X)}
    place.update({X + k: X + k for k in range(4)})
    place.update({-1: X + 4, -2: X + 5, -3: X + 6})
    s2 = {n: unit[place[2 * n]] * BALANCE for n in range(-1, n_all + 2)}
    d2 = {n: unit[place[2 * n + 1]] / BALANCE for n in range(-2, n_all + 2)}
    s1 = {n: s2[n] - UPDATE_SECOND * (d2[n - 1] + d2[n]) for n in range(-1, n_all + 2)}
    d1 = {n: d2[n] - PREDICT_SECOND * (s1[n] + s1[n + 1]) for n in range(-1, n_all + 1)}
    s = {n: s1[n] - UPDATE_FIRST * (d1[n - 1] + d1[n]) for n in range(n_all + 1)}
    d = {n: d1[n] - PREDICT_FIRST * (s[n] + s[n + 1]) for n in range(n_all)}
    out = np.zeros((2 * X, X))
    for n in range(n_all):
        out[:, 2 * n] = s[n]
        out[:, 2 * n + 1] = d[n]
    return out


def whole(shape):
    return pl.BlockSpec(memory_space=pltpu.VMEM)


def call(kernel, out_shape, n_in, scratch=(), name=None, smem=()):
    return pl.pallas_call(
        kernel,
        out_shape=out_shape,
        in_specs=[
            pl.BlockSpec(memory_space=pltpu.SMEM if i in smem else pltpu.VMEM) for i in range(n_in)
        ],
        out_specs=jax.tree.map(lambda _: pl.BlockSpec(memory_space=pltpu.VMEM), out_shape),
        scratch_shapes=list(scratch),
        compiler_params=pltpu.CompilerParams(vmem_limit_bytes=VMEM_LIMIT),
        name=name,
    )


def fill_line(source, line, ny):
    def body(k, carry):
        at = pl.multiple_of(k * 256, 256)
        line[pl.ds(MARGIN + at, 256), :] = source[pl.ds(at, 256), :]
        return carry

    lax.fori_loop(0, ny // 256, body, 0)
    for k in range(1, 9):
        line[pl.ds(MARGIN - k, 1), :] = line[pl.ds(MARGIN + k, 1), :]
        line[pl.ds(MARGIN + ny - 1 + k, 1), :] = line[pl.ds(MARGIN + ny - 1 - k, 1), :]


def after(rows):
    return pltpu.roll(rows, rows.shape[0] - 1, 0)


def before(rows):
    return pltpu.roll(rows, 1, 0)


def lift_rows(line, target, ny, forward):
    cells = 128
    pairs = cells // 2
    wide = pairs + 8

    def body(k, carry):
        at = pl.multiple_of(k * cells, cells)
        s = line[pl.ds(MARGIN + at - 8, wide, stride=2), :]
        d = line[pl.ds(MARGIN + at - 7, wide, stride=2), :]
        if forward:
            d = d + PREDICT_FIRST * (s + after(s))
            s = s + UPDATE_FIRST * (before(d) + d)
            d = d + PREDICT_SECOND * (s + after(s))
            s = s + UPDATE_SECOND * (before(d) + d)
            s = s * (1.0 / BALANCE)
            d = d * BALANCE
        else:
            s = s * BALANCE
            d = d * (1.0 / BALANCE)
            s = s - UPDATE_SECOND * (before(d) + d)
            d = d - PREDICT_SECOND * (s + after(s))
            s = s - UPDATE_FIRST * (before(d) + d)
            d = d - PREDICT_FIRST * (s + after(s))
        target[pl.ds(at, pairs, stride=2), :] = s[4 : 4 + pairs]
        target[pl.ds(at + 1, pairs, stride=2), :] = d[4 : 4 + pairs]
        return carry

    lax.fori_loop(0, ny // cells, body, 0, unroll=2)


def column_kernel(forward, source, target, line):
    ny = source.shape[0]
    fill_line(source, line, ny)
    lift_rows(line, target, ny, forward)


def columns(values, forward):
    ny = values.shape[0]
    return call(
        functools.partial(column_kernel, forward),
        jax.ShapeDtypeStruct((ny, X), jnp.float32),
        1,
        [pltpu.VMEM((ny + 2 * MARGIN, X), jnp.float32)],
        "analyse_y" if forward else "synthesise_y",
    )(values)


def edge_kernel(values, weights, to_left, to_right):
    edges = lax.dot_general(
        weights[...], values[...], (((1,), (1,)), ((), ())),
        precision=lax.Precision.HIGHEST, preferred_element_type=jnp.float32,
    )
    to_left[...] = edges[0:4]
    to_right[...] = edges[4:8]


def edges_of(values, weights):
    cells = values.shape[0]
    half = jax.ShapeDtypeStruct((4, cells), jnp.float32)
    return call(edge_kernel, (half, half), 2, name="edges_x")(values, weights)


def lift_depth(cells, gain_low, gain_high):
    n = len(cells) // 2
    s, d = cells[0::2], cells[1::2]

    def right(list_, k):
        return list_[k + 1] if k + 1 < n else list_[n - 1]

    def left(list_, k):
        return list_[k - 1] if k > 0 else list_[0]

    d = [d[k] + PREDICT_FIRST * (s[k] + right(s, k)) for k in range(n)]
    s = [s[k] + UPDATE_FIRST * (left(d, k) + d[k]) for k in range(n)]
    d = [d[k] + PREDICT_SECOND * (s[k] + right(s, k)) for k in range(n)]
    s = [s[k] + UPDATE_SECOND * (left(d, k) + d[k]) for k in range(n)]
    low = [v * (1.0 / BALANCE) for v in s]
    high = [v * BALANCE for v in d]
    s = [v * gain_low for v in s]
    d = [v * gain_high for v in d]
    s = [s[k] - UPDATE_SECOND * (left(d, k) + d[k]) for k in range(n)]
    d = [d[k] - PREDICT_SECOND * (s[k] + right(s, k)) for k in range(n)]
    s = [s[k] - UPDATE_FIRST * (left(d, k) + d[k]) for k in range(n)]
    d = [d[k] - PREDICT_FIRST * (s[k] + right(s, k)) for k in range(n)]
    coefficients = [v for pair in zip(low, high) for v in pair]
    rebuilt = [v for pair in zip(s, d) for v in pair]
    return coefficients, rebuilt


def gain_tables(gains, x_odd):
    y_odd = lax.broadcasted_iota(jnp.int32, (ROWS, X), 0) % 2 == 1
    tables = []
    for z in range(2):
        low = jnp.where(x_odd, gains[4 * z + 1], gains[4 * z])
        high = jnp.where(x_odd, gains[4 * z + 3], gains[4 * z + 2])
        tables.append(jnp.where(y_odd, high, low))
    return tables


def depth_kernel(values, from_right, from_left, gains, forward, backward, coefficients, rebuilt, halo):
    nz, ny, _ = values.shape
    cells = nz * ny
    for at in range(0, cells, X):
        both = jnp.concatenate([from_right[:, at : at + X], from_left[:, at : at + X]], 0)
        both = jnp.concatenate([both, jnp.zeros((X - HALO, X), jnp.float32)], 0)
        z, y = at // ny, at % ny
        turned = both.T
        if ny >= X:
            halo[z, y : y + X, :] = turned
        else:
            for k in range(X // ny):
                halo[z + k, :, :] = turned[k * ny : (k + 1) * ny]
    lane = lax.broadcasted_iota(jnp.int32, (ROWS, X), 1)
    inner = gain_tables(gains, lane % 2 == 1)
    beyond = gain_tables(gains, ((lane < 4) & (lane % 2 == 1)) | ((lane >= 4) & (lane % 2 == 0)))

    def body(k, carry):
        rows = pl.ds(pl.multiple_of(k * ROWS, ROWS), ROWS)
        inside = values[:, rows, :].reshape(nz * ROWS, X)
        outside = halo[:, rows, :].reshape(nz * ROWS, X)
        lines = jnp.dot(
            jnp.concatenate([inside, outside], 1), forward[...],
            precision=lax.Precision.HIGHEST, preferred_element_type=jnp.float32,
        )
        parts = []
        for part, tables in ((0, inner), (1, beyond)):
            cut = lines[:, part * X : (part + 1) * X]
            registers = [cut[z * ROWS : (z + 1) * ROWS] for z in range(nz)]
            found, again = lift_depth(registers, *tables)
            if part == 0:
                for z in range(nz):
                    coefficients[z, rows, :] = found[z]
            parts.append(jnp.concatenate(again, 0))
        lines = jnp.dot(
            jnp.concatenate(parts, 1), backward[...],
            precision=lax.Precision.HIGHEST, preferred_element_type=jnp.float32,
        )
        rebuilt[:, rows, :] = lines.reshape(nz, ROWS, X)
        return carry

    lax.fori_loop(0, ny // ROWS, body, 0)


def depths(values, from_right, from_left, gains, forward, backward):
    shape = jax.ShapeDtypeStruct(values.shape, jnp.float32)
    return call(
        depth_kernel, (shape, shape), 6, [pltpu.VMEM(values.shape, jnp.float32)], "depth", smem=(3,)
    )(values, from_right, from_left, gains, forward, backward)


def per_device(blocks, field, gains):
    f32 = jnp.float32
    index = lax.axis_index("ba")
    forward = jnp.where(
        index == 0,
        jnp.asarray(analysis_matrix(True, blocks == 1), f32),
        jnp.where(
            index == blocks - 1,
            jnp.asarray(analysis_matrix(False, True), f32),
            jnp.asarray(analysis_matrix(False, False), f32),
        ),
    )
    backward = jnp.asarray(synthesis_matrix(), f32)
    edge_weights = jnp.asarray(edge_matrix(), f32)

    nz = lax.axis_size("aa")
    ny = field.shape[1]
    by_lines = columns(field.reshape(ny, X), True)
    by_depth = lax.all_to_all(by_lines.reshape(nz, ny // nz, X), "aa", 0, 0, tiled=True)
    to_left, to_right = edges_of(by_depth.reshape(ny, X), edge_weights)
    from_right = lax.ppermute(to_left, "ba", [(k, k - 1) for k in range(1, blocks)])
    from_left = lax.ppermute(to_right, "ba", [(k, k + 1) for k in range(blocks - 1)])
    coefficients, rebuilt = depths(
        by_depth, from_right, from_left, gains.reshape(8), forward, backward
    )
    rebuilt = lax.all_to_all(rebuilt, "aa", 0, 0, tiled=True)
    rebuilt = columns(rebuilt.reshape(ny, X), False)
    return coefficients, rebuilt.reshape(1, ny, X)


def solution(mesh):
    return jax.shard_map(
        functools.partial(per_device, mesh.shape["ba"]),
        mesh=mesh,
        in_specs=(P("aa", None, "ba"), P()),
        out_specs=(P(None, "aa", "ba"), P("aa", None, "ba")),
        check_vma=False,
    )
```

time: 267 us -> 100 us (0.37)
  the two profiles are of different devices: /device:TPU:184 before, /device:TPU:256 now
where the time goes in v1:
time: 100 us; the launch traced here: 99.8 us
  waiting for transfers between devices  33.9 us (34%)
  blocking collectives  31.5 us (32%)
  starting transfers between devices  17.6 us (18%)
  Pallas kernels  14.6 us (15%)
  local copies, waits for them, and re-layouts  1.33 us (1%)
    all_to_all x1, blocking collectives, per_device(): rebuilt = lax.all_to_all(rebuilt, 'aa', 0, 0, tiled=True)  31.5 us
    all_to_all x1, waiting for transfers between devices, per_device(): lax.all_to_all(by_lines.reshape(nz, ny // nz, X), 'aa', 0, 0, tiled=True)  27.9 us
    pallas_call x1, Pallas kernels, depths(): call(depth_kernel, (shape, shape), 6, [pltpu.VMEM(values.shape, jnp.float...  10.4 us
    all_to_all x1, starting transfers between devices, per_device(): lax.all_to_all(by_lines.reshape(nz, ny // nz, X), 'aa', 0, 0, tiled=True)  7.73 us
    ppermute x1, waiting for transfers between devices, per_device(): lax.ppermute(to_right, 'ba', [(k, k + 1) for k in range(blocks - 1)])  6.01 us
    ppermute x1, starting transfers between devices, per_device(): lax.ppermute(to_right, 'ba', [(k, k + 1) for k in range(blocks - 1)])  5.76 us
    ppermute x1, starting transfers between devices, per_device(): lax.ppermute(to_left, 'ba', [(k, k - 1) for k in range(1, blocks)])  4.13 us
    pallas_call x2, Pallas kernels, columns(): call(functools.partial(column_kernel, forward), jax.ShapeDtypeStruct((ny,...  3.23 us
  transfers between devices with their start and end apart: 3, of which 2 were waited for; matrix products, arithmetic and copies ran while one was open for 0% of the time, Pallas kernels for 0%

profile of v1, /device:TPU:256, one launch (start us, length us, event | category | flops | bytes accessed | tf_op | source)
XLA Modules:
  0.0 99.8 jit_solution(8783395476407150757)
XLA Ops:
  0.6 0.0 copy-start
  0.6 1.2 %copy-done = f32[1,2048,128]{2,1,0:T(8,128)S(1)} copy-done((f32[1,2048,128]{2,1,0:T(8,128)S(1)}, f32[1,2048,128]{2,1,0:T(8,128)}, u32[]{:S(2)}) %copy-start) | copy-done | bytes 1048600
  1.9 1.6 %analyse_y.1 = f32[2048,128]{1,0:T(8,128)} custom-call(f32[2048,128]{1,0:T(8,128)S(1)} %bitcast.7), custom_call_target="tpu_custom_call" | custom-call | tf_op jit(solution)/shard_map/analyse_y/pallas_call | solution.py:167
  3.5 7.7 %all-to-all-start = ((f32[32,64,128]{2,1,0:T(8,128)}), f32[32,64,128]{2,1,0:T(8,128)S(1)}, u32[]{:S(2)}, u32[]{:S(2)}) async-start(f32[32,64,128]{2,1,0:T(8,128)} %bitcast.1), calls=%async_computation | async-start | bytes 2097152 | tf_op jit(solution)/shard_map/all_to_all | solution.py:297
  11.2 0.0 copy-start.2
  11.2 27.9 %all-to-all-done.values = f32[32,64,128]{2,1,0:T(8,128)S(1)} async-done(((f32[32,64,128]{2,1,0:T(8,128)}), f32[32,64,128]{2,1,0:T(8,128)S(1)}, u32[]{:S(2)}, u32[]{:S(2)}) %all-to-all-start) | async-done | bytes 1048608 | tf_op jit(solution)/shard_map/all_to_all | solution.py:297
  39.2 0.0 copy-done.2
  39.2 0.0 copy-start.3
  39.2 0.0 copy-start.4
  39.2 0.0 copy-start.5
  39.2 0.9 edges_x.1
  40.1 4.1 %collective-permute-start = (f32[4,2048]{1,0:T(4,128)S(1)}, f32[4,2048]{1,0:T(4,128)S(1)}, u32[]{:S(2)}, u32[]{:S(2)}) collective-permute-start(f32[4,2048]{1,0:T(4,128)S(1)} %get-tuple-element.6), channel_id=1, source_target_pairs={{1,0},{2,1},{3,2},{4,3},{5,4},{6,5},{7,6},{8,7},{9,8},{10,9},{11,1... | collective-permute-start | bytes 98312 | tf_op jit(solution)/shard_map/ppermute | solution.py:299
  44.2 0.0 copy-start.6
  44.3 0.0 copy-start.1
  44.3 5.8 %collective-permute-start.1 = (f32[4,2048]{1,0:T(4,128)S(1)}, f32[4,2048]{1,0:T(4,128)S(1)}, u32[]{:S(2)}, u32[]{:S(2)}) collective-permute-start(f32[4,2048]{1,0:T(4,128)S(1)} %get-tuple-element.7), channel_id=1, source_target_pairs={{0,1},{1,2},{2,3},{3,4},{4,5},{5,6},{6,7},{7,8},{8,9},{9,10},{10,1... | collective-permute-start | bytes 98312 | tf_op jit(solution)/shard_map/ppermute | solution.py:300
  50.0 0.0 copy-done.3
  50.0 0.0 copy-done.4
  50.0 0.0 copy-done.5
  50.1 0.1 select_select_fusion.forward
  50.1 0.0 copy-done.6
  50.1 0.1 reshape.25.gains
  50.2 0.0 collective-permute-done.from_right
  50.2 6.0 %collective-permute-done.1.from_left = f32[4,2048]{1,0:T(4,128)S(1)} collective-permute-done((f32[4,2048]{1,0:T(4,128)S(1)}, f32[4,2048]{1,0:T(4,128)S(1)}, u32[]{:S(2)}, u32[]{:S(2)}) %collective-permute-start.1) | collective-permute-done | bytes 32800 | tf_op jit(solution)/shard_map/ppermute | solution.py:300
  56.2 0.0 copy-done.1
  56.2 10.4 %depth.1 = (f32[32,64,128]{2,1,0:T(8,128)}, f32[32,64,128]{2,1,0:T(8,128)S(1)}) custom-call(f32[32,64,128]{2,1,0:T(8,128)S(1)} %all-to-all-done.values, f32[4,2048]{1,0:T(4,128)S(1)} %collective-permute-done.from_right, f32[4,2048]{1,0:T(4,128)S(1)} %collective-permute-done.1.from_left, f32[8]{0:T(128)S(1)} %reshape.25.gains, ...), custom_call_target="tpu_custom_call" | custom-call | tf_op jit(solution)/shard_map/depth/pallas_call | solution.py:274
  66.6 31.5 %all_to_all.10 = f32[32,64,128]{2,1,0:T(8,128)S(1)} all-to-all(f32[32,64,128]{2,1,0:T(8,128)S(1)} %get-tuple-element.9), channel_id=1, replica_groups=mesh['aa'=32,'ba'=16] {'aa'}, dimensions={0} | all-to-all | bytes 2097152 | tf_op jit(solution)/shard_map/all_to_all | solution.py:304
  98.2 1.6 %synthesise_y.1 = f32[2048,128]{1,0:T(8,128)} custom-call(f32[2048,128]{1,0:T(8,128)S(1)} %bitcast.6), custom_call_target="tpu_custom_call" | custom-call | tf_op jit(solution)/shard_map/synthesise_y/pallas_call | solution.py:167
Async XLA Ops:
  0.6 1.2 %copy-start = (f32[1,2048,128]{2,1,0:T(8,128)S(1)}, f32[1,2048,128]{2,1,0:T(8,128)}, u32[]{:S(2)}) copy-start(f32[1,2048,128]{2,1,0:T(8,128)} %param.7) | copy-start | bytes 3145732
  3.5 35.7 %all-to-all-start = ((f32[32,64,128]{2,1,0:T(8,128)}), f32[32,64,128]{2,1,0:T(8,128)S(1)}, u32[]{:S(2)}, u32[]{:S(2)}) async-start(f32[32,64,128]{2,1,0:T(8,128)} %bitcast.1), calls=%async_computation | async-start | bytes 2097152 | tf_op jit(solution)/shard_map/all_to_all | solution.py:297
  11.2 28.0 %copy-start.2 = (f32[8,128]{1,0:T(8,128)S(1)}, f32[8,128]{1,0:T(8,128)}, u32[]{:S(2)}) copy-start(f32[8,128]{1,0:T(8,128)} %constant.22.clone.weights) | copy-start | bytes 12292
  39.2 10.9 %copy-start.3 = (f32[256,256]{1,0:T(8,128)S(1)}, f32[256,256]{1,0:T(8,128)}, u32[]{:S(2)}) copy-start(f32[256,256]{1,0:T(8,128)} %constant.20.clone) | copy-start | bytes 786436
  39.2 10.9 %copy-start.4 = (f32[256,256]{1,0:T(8,128)S(1)}, f32[256,256]{1,0:T(8,128)}, u32[]{:S(2)}) copy-start(f32[256,256]{1,0:T(8,128)} %constant.19.clone) | copy-start | bytes 786436
  39.2 10.9 %copy-start.5 = (f32[256,256]{1,0:T(8,128)S(1)}, f32[256,256]{1,0:T(8,128)}, u32[]{:S(2)}) copy-start(f32[256,256]{1,0:T(8,128)} %constant.18.clone) | copy-start | bytes 786436
  40.1 10.1 %collective-permute-start = (f32[4,2048]{1,0:T(4,128)S(1)}, f32[4,2048]{1,0:T(4,128)S(1)}, u32[]{:S(2)}, u32[]{:S(2)}) collective-permute-start(f32[4,2048]{1,0:T(4,128)S(1)} %get-tuple-element.6), channel_id=1, source_target_pairs={{1,0},{2,1},{3,2},{4,3},{5,4},{6,5},{7,6},{8,7},{9,8},{10,9},{11,1... | collective-permute-start | bytes 98312 | tf_op jit(solution)/shard_map/ppermute | solution.py:299
  44.2 5.9 %copy-start.6 = (f32[2,2,2]{2,1,0:T(2,128)S(1)}, f32[2,2,2]{2,1,0:T(2,128)}, u32[]{:S(2)}) copy-start(f32[2,2,2]{2,1,0:T(2,128)} %param.8) | copy-start | bytes 100
  44.3 12.0 %copy-start.1 = (f32[256,128]{1,0:T(8,128)S(1)}, f32[256,128]{1,0:T(8,128)}, u32[]{:S(2)}) copy-start(f32[256,128]{1,0:T(8,128)} %constant.21.clone.backward) | copy-start | bytes 393220
  44.3 12.0 %collective-permute-start.1 = (f32[4,2048]{1,0:T(4,128)S(1)}, f32[4,2048]{1,0:T(4,128)S(1)}, u32[]{:S(2)}, u32[]{:S(2)}) collective-permute-start(f32[4,2048]{1,0:T(4,128)S(1)} %get-tuple-element.7), channel_id=1, source_target_pairs={{0,1},{1,2},{2,3},{3,4},{4,5},{5,6},{6,7},{7,8},{8,9},{9,10},{10,1... | collective-permute-start | bytes 98312 | tf_op jit(solution)/shard_map/ppermute | solution.py:300

commit v2 on v0

v2 whole, which is shorter than its diff:
```python
import functools

import jax
import jax.numpy as jnp
import numpy as np
from jax import lax
from jax.experimental import pallas as pl
from jax.experimental.pallas import tpu as pltpu
from jax.sharding import PartitionSpec as P

PREDICT_FIRST = -1.586134342059924
UPDATE_FIRST = -0.052980118572961
PREDICT_SECOND = 0.882911075530934
UPDATE_SECOND = 0.443506852043971
BALANCE = 1.230174104914001
A, B, C, E = PREDICT_FIRST, UPDATE_FIRST, PREDICT_SECOND, UPDATE_SECOND

X = 128
HALF = X // 2
ROWS = 8
MARGIN = 16
CHUNK = 256
VMEM_LIMIT = 24 * 1024 * 1024
EDGE = 8
HIGHEST = lax.Precision.HIGHEST


def edge_matrix():
    unit = np.eye(X)
    s, d = unit[0::2], unit[1::2]
    d1 = [d[n] + A * (s[n] + s[n + 1]) for n in range(HALF - 1)]
    s1 = [None] + [s[n] + B * (d1[n - 1] + d1[n]) for n in range(1, HALF - 1)]
    last = HALF - 1
    out = np.zeros((16, X))
    out[0] = s[0]
    out[1] = d1[0]
    out[2] = s1[1]
    out[3] = d1[1] + C * (s1[1] + s1[2])
    out[4] = d[last] + A * s[last]
    out[5] = s[last] + B * d1[last - 1]
    out[6] = d1[last - 1] + C * s1[last - 1]
    out[8] = d[0] + A * s[1]
    out[9] = s[1] + B * d1[1]
    out[10] = d1[1] + C * s1[2]
    out[12] = s[last]
    out[13] = d1[last - 1]
    out[14] = s1[last - 1]
    out[15] = d1[last - 2] + C * (s1[last - 2] + s1[last - 1])
    return np.concatenate([out[:, :EDGE], out[:, X - EDGE :]], 1)


def correction_matrix(left_end, right_end):
    unit = np.eye(24)
    own = unit[8:]
    h0, h1, h2, h3 = own[12:16] if right_end else unit[0:4]
    hp, hq, hr = own[8:11] if left_end else unit[4:7]
    s0, d10, p, q = own[0], own[1], own[4], own[5]
    add_d1 = A * h0
    d1 = p + add_d1
    s1_next = h0 + B * (d1 + h1)
    add_s1 = B * add_d1
    add_d2 = add_d1 + C * (add_s1 + s1_next)
    add_d2_before = C * add_s1
    add_s2 = add_s1 + E * (add_d2_before + add_d2)
    add_s2_before = E * add_d2_before
    s1 = q + B * d1
    d2 = d1 + C * (s1 + s1_next)
    d2_next = h1 + C * (s1_next + h2)
    s2_next = s1_next + E * (d2 + d2_next)
    s2_after = h2 + E * (d2_next + h3)
    right = [add_s2_before, add_d2_before, add_s2, add_d2]
    right_beyond = [s2_next, d2_next, s2_after, h3]
    d1_out = hp + A * s0
    s1_out = hq + B * d1_out
    add_s1 = B * d1_out
    s1 = s0 + B * (d1_out + d10)
    add_d2 = C * add_s1
    d2_out = d1_out + C * (s1_out + s1)
    d2_far = hr + C * s1_out
    s2_out = s1_out + E * (d2_far + d2_out)
    left = [add_s1 + E * (d2_out + add_d2), add_d2, E * add_d2, 0 * s0]
    left_beyond = [d2_out, s2_out, d2_far, 0 * s0]
    found = np.stack(left + right + right_beyond + left_beyond)
    return np.concatenate([found[:, :8], found[:, 8:] @ edge_matrix()], 1)


def own_analysis_matrix():
    unit = np.eye(X)
    zero = np.zeros((1, X))
    s, d = unit[0::2], unit[1::2]
    d = d + A * (s + np.concatenate([s[1:], zero]))
    s = s + B * (d + np.concatenate([zero, d[:-1]]))
    d = d + C * (s + np.concatenate([s[1:], zero]))
    s = s + E * (d + np.concatenate([zero, d[:-1]]))
    out = np.zeros((X, X))
    out[:, 0::2] = s.T
    out[:, 1::2] = d.T
    return out


def synthesis_matrix():
    unit = np.eye(X + 8)
    place = {k: k for k in range(X + 4)}
    place.update({-1: X + 4, -2: X + 5, -3: X + 6})
    n_all = HALF
    s2 = {n: unit[place[2 * n]] for n in range(-1, n_all + 2)}
    d2 = {n: unit[place[2 * n + 1]] for n in range(-2, n_all + 2)}
    s1 = {n: s2[n] - E * (d2[n - 1] + d2[n]) for n in range(-1, n_all + 2)}
    d1 = {n: d2[n] - C * (s1[n] + s1[n + 1]) for n in range(-1, n_all + 1)}
    s = {n: s1[n] - B * (d1[n - 1] + d1[n]) for n in range(n_all + 1)}
    d = {n: d1[n] - A * (s[n] + s[n + 1]) for n in range(n_all)}
    cells = np.zeros((X, X + 8))
    cells[0::2] = [s[n] for n in range(n_all)]
    cells[1::2] = [d[n] for n in range(n_all)]
    return cells


def edge_synthesis_matrix():
    inside = [0, 1, 2, 3, 124, 125, 126, 127] + [X + k for k in range(8)]
    return synthesis_matrix()[list(range(8)) + list(range(120, 128))][:, inside]


def call(kernel, out_shape, spaces, scratch=(), name=None, out_space=pltpu.VMEM, cost=None):
    if isinstance(out_space, tuple):
        out_specs = tuple(pl.BlockSpec(memory_space=space) for space in out_space)
    else:
        out_specs = jax.tree.map(lambda _: pl.BlockSpec(memory_space=out_space), out_shape)
    return pl.pallas_call(
        kernel,
        out_shape=out_shape,
        in_specs=[pl.BlockSpec(memory_space=space) for space in spaces],
        out_specs=out_specs,
        scratch_shapes=list(scratch),
        compiler_params=pltpu.CompilerParams(vmem_limit_bytes=VMEM_LIMIT),
        cost_estimate=cost,
        name=name,
    )


def array(*shape):
    return jax.ShapeDtypeStruct(shape, jnp.float32)


def after(rows):
    return pltpu.roll(rows, rows.shape[0] - 1, 0)


def before(rows):
    return pltpu.roll(rows, 1, 0)


def lift_rows(line, target, at, forward):
    cells = 128
    pairs = cells // 2
    wide = pairs + 8
    s = line[pl.ds(MARGIN + at - 8, wide, stride=2), :]
    d = line[pl.ds(MARGIN + at - 7, wide, stride=2), :]
    if forward:
        d = d + A * (s + after(s))
        s = s + B * (before(d) + d)
        d = d + C * (s + after(s))
        s = s + E * (before(d) + d)
        s = s * (1.0 / BALANCE)
        d = d * BALANCE
    else:
        s = s * BALANCE
        d = d * (1.0 / BALANCE)
        s = s - E * (before(d) + d)
        d = d - C * (s + after(s))
        s = s - B * (before(d) + d)
        d = d - A * (s + after(s))
    target[pl.ds(at, pairs, stride=2), :] = s[4 : 4 + pairs]
    target[pl.ds(at + 1, pairs, stride=2), :] = d[4 : 4 + pairs]


def mirror_start(line):
    for k in range(1, 9):
        line[pl.ds(MARGIN - k, 1), :] = line[pl.ds(MARGIN + k, 1), :]


def mirror_end(line, ny):
    for k in range(1, 9):
        line[pl.ds(MARGIN + ny - 1 + k, 1), :] = line[pl.ds(MARGIN + ny - 1 - k, 1), :]


def analyse_kernel(source, target, line, arrived):
    ny = source.shape[0]
    n = ny // CHUNK
    copies = []
    for k in range(n):
        inner = pl.ds(MARGIN + k * CHUNK, CHUNK)
        rows = pl.ds(k * CHUNK, CHUNK)
        copies.append(pltpu.make_async_copy(source.at[rows], line.at[inner], arrived.at[k]))
        copies[k].start()
    copies[0].wait()
    mirror_start(line)
    for k in range(n):
        if k + 1 < n:
            copies[k + 1].wait()
        else:
            mirror_end(line, ny)
        for at in range(k * CHUNK, (k + 1) * CHUNK, 128):
            lift_rows(line, target, at, True)


def analyse_columns(values):
    ny = values.shape[0]
    scratch = [
        pltpu.VMEM((ny + 2 * MARGIN, X), jnp.float32),
        pltpu.SemaphoreType.DMA((ny // CHUNK,)),
    ]
    return call(analyse_kernel, pltpu.VMEM((ny, X), jnp.float32), [pltpu.HBM], scratch, "analyse_y")(pltpu.with_memory_space_constraint(values, pltpu.HBM))


def synthesise_kernel(source, target, line, lifted, left):
    ny = source.shape[0]
    n = ny // CHUNK
    for k in range(n):
        line[pl.ds(MARGIN + k * CHUNK, CHUNK), :] = source[pl.ds(k * CHUNK, CHUNK), :]
    mirror_start(line)
    mirror_end(line, ny)
    copies = []
    for k in range(n):
        for at in range(k * CHUNK, (k + 1) * CHUNK, 128):
            lift_rows(line, lifted, at, False)
        rows = pl.ds(k * CHUNK, CHUNK)
        copies.append(pltpu.make_async_copy(lifted.at[rows], target.at[rows], left.at[k]))
        copies[k].start()
    for copy in copies:
        copy.wait()


def synthesise_columns(values):
    ny = values.shape[0]
    scratch = [
        pltpu.VMEM((ny + 2 * MARGIN, X), jnp.float32),
        pltpu.VMEM((ny, X), jnp.float32),
        pltpu.SemaphoreType.DMA((ny // CHUNK,)),
    ]
    return call(
        synthesise_kernel, array(ny, X), [pltpu.VMEM], scratch, "synthesise_y", pltpu.HBM
    )(values)


def edge_kernel(values, to_left, to_right, edges):
    cells = values.shape[0]
    for at in range(0, cells, X):
        turned = values[pl.ds(at, X), :].T
        edges[0:EDGE, pl.ds(at, X)] = turned[:EDGE]
        edges[EDGE : 2 * EDGE, pl.ds(at, X)] = turned[X - EDGE :]

    def cell(k):
        return edges[pl.ds(k, 1), :]

    s = [cell(2 * n) for n in range(EDGE)]
    d = [cell(2 * n + 1) for n in range(EDGE)]
    d1 = {n: d[n] + A * (s[n] + s[n + 1]) for n in (0, 1, 2, 5, 6)}
    s1 = {n: s[n] + B * (d1[n - 1] + d1[n]) for n in (1, 2, 6)}
    to_left[0:1] = s[0]
    to_left[1:2] = d1[0]
    to_left[2:3] = s1[1]
    to_left[3:4] = d1[1] + C * (s1[1] + s1[2])
    to_right[0:1] = d[7] + A * s[7]
    to_right[1:2] = s[7] + B * d1[6]
    to_right[2:3] = d1[6] + C * s1[6]
    to_right[3:4] = jnp.zeros_like(s[0])


def edges_of(values):
    cells = values.shape[0]
    shapes = (array(4, cells), array(4, cells), array(2 * EDGE, cells))
    return call(edge_kernel, shapes, [pltpu.VMEM], name="edges_x")(values)


def analyse_depth(cells):
    n = len(cells) // 2
    s, d = cells[0::2], cells[1::2]

    def right(k):
        return s[min(k + 1, n - 1)]

    def left(k):
        return d[max(k - 1, 0)]

    d = [d[k] + A * (s[k] + right(k)) for k in range(n)]
    s = [s[k] + B * (left(k) + d[k]) for k in range(n)]
    d = [d[k] + C * (s[k] + right(k)) for k in range(n)]
    s = [s[k] + E * (left(k) + d[k]) for k in range(n)]
    return s, d


def synthesise_depth(s, d):
    n = len(s)

    def right(k):
        return s[min(k + 1, n - 1)]

    def left(k):
        return d[max(k - 1, 0)]

    s = [s[k] - E * (left(k) + d[k]) for k in range(n)]
    d = [d[k] - C * (s[k] + right(k)) for k in range(n)]
    s = [s[k] - B * (left(k) + d[k]) for k in range(n)]
    d = [d[k] - A * (s[k] + right(k)) for k in range(n)]
    return [v for pair in zip(s, d) for v in pair]


def gain_tables(gains, y_odd, x_odd):
    tables = []
    for z in range(2):
        low = jnp.where(x_odd, gains[z, 0, 1], gains[z, 0, 0])
        high = jnp.where(x_odd, gains[z, 1, 1], gains[z, 1, 0])
        tables.append(jnp.where(y_odd, high, low))
    return tables


def scale_tables(x_odd):
    along = jnp.where(x_odd, BALANCE, 1.0 / BALANCE)
    return along * (1.0 / BALANCE), along * BALANCE


def dot(left, right):
    return jnp.dot(left, right, precision=lax.Precision.HIGHEST, preferred_element_type=jnp.float32)


def main_kernel(values, gains, edges, forward, backward, coefficients, rebuilt):
    del edges
    nz, ny, _ = values.shape
    lane = lax.broadcasted_iota(jnp.int32, (ROWS, X), 1)
    row = lax.broadcasted_iota(jnp.int32, (ROWS, X), 0)
    gain_low, gain_high = gain_tables(gains, row % 2 == 1, lane % 2 == 1)
    scale_low, scale_high = scale_tables(lane % 2 == 1)
    rebuilt[...] = dot(values[...].reshape(nz * ny, X), forward[...]).reshape(nz, ny, X)

    def body(k, carry):
        rows = pl.ds(pl.multiple_of(k * ROWS, ROWS), ROWS)
        s, d = analyse_depth([rebuilt[z, rows, :] for z in range(nz)])
        for n in range(nz // 2):
            coefficients[2 * n, rows, :] = s[n] * scale_low
            coefficients[2 * n + 1, rows, :] = d[n] * scale_high
        cells = synthesise_depth([v * gain_low for v in s], [v * gain_high for v in d])
        for z in range(nz):
            rebuilt[z, rows, :] = cells[z]
        return carry

    lax.fori_loop(0, ny // ROWS, body, 0)
    rebuilt[...] = dot(rebuilt[...].reshape(nz * ny, X), backward[...]).reshape(nz, ny, X)


def main_depths(values, gains, edges):
    shape = array(*values.shape)
    size = values.size
    cost = pl.CostEstimate(flops=100 * size, bytes_accessed=12 * size, transcendentals=0)
    spaces = [pltpu.VMEM, pltpu.SMEM, pl.ANY, pltpu.VMEM, pltpu.VMEM]
    forward = jnp.asarray(own_analysis_matrix(), jnp.float32)
    backward = jnp.asarray(synthesis_matrix()[:, :X].T, jnp.float32)
    return call(main_kernel, (shape, shape), spaces, name="depth_main", cost=cost)(
        values, gains, edges, forward, backward
    )


def halo_kernel(
    blocks, own_rebuilt, from_right, from_left, edges, gains, weights, spread, rebuilt, added, held, left
):
    nz = own_rebuilt.shape[0]
    index = lax.axis_index("ba")
    kind = 2 * (index == 0).astype(jnp.int32) + (index == blocks - 1).astype(jnp.int32)
    halo = jnp.concatenate([from_right[...], from_left[...], edges[...]], 0)
    found = dot(weights[kind], halo)
    lane = lax.broadcasted_iota(jnp.int32, (ROWS, X), 1)
    row = lax.broadcasted_iota(jnp.int32, (ROWS, X), 0)
    low = lane < HALF
    low_16 = lax.broadcasted_iota(jnp.int32, (16, X), 1) < HALF
    cells = []
    for k in range(nz // 2):
        inside = found[0:8, k * X : (k + 1) * X]
        beyond = found[8:16, k * X : (k + 1) * X]
        cells.append(jnp.where(low, inside, pltpu.roll(beyond, HALF, 1)))
        cells.append(jnp.where(low, pltpu.roll(inside, HALF, 1), beyond))
    x_odd = (row + jnp.where(low | (row < 4), 0, 1)) % 2 == 1
    gain_low, gain_high = gain_tables(gains, lane % 2 == 1, x_odd)
    scale_low, scale_high = scale_tables(x_odd)
    s, d = analyse_depth(cells)
    for n in range(nz // 2):
        added[2 * n] = s[n] * scale_low
        added[2 * n + 1] = d[n] * scale_high
    copies = []
    cells = synthesise_depth([v * gain_low for v in s], [v * gain_high for v in d])
    table = [spread[:, k * X : (k + 1) * X] for k in range(8)]
    middle = jnp.zeros((X - 16, X), jnp.float32)
    for k in range(nz // 2):
        mixed = []
        for v in cells[2 * k : 2 * k + 2]:
            total = None
            for m in range(8):
                term = table[m] * jnp.broadcast_to(v[m : m + 1], (16, X))
                total = term if total is None else total + term
            mixed.append(total + pltpu.roll(total, HALF, 1))
        both = jnp.where(low_16, *mixed)
        turned = jnp.concatenate([both[:8], middle, both[8:]], 0).T
        held[2 * k] = own_rebuilt[2 * k] + turned[:HALF]
        held[2 * k + 1] = own_rebuilt[2 * k + 1] + turned[HALF:]
        if k % 2 == 1:
            part = pl.ds(2 * k - 2, 4)
            copies.append(pltpu.make_async_copy(held.at[part], rebuilt.at[part], left.at[k // 2]))
            copies[-1].start()
    for copy in copies:
        copy.wait()


def add_halo(blocks, own_rebuilt, from_right, from_left, edges, gains):
    nz = own_rebuilt.shape[0]
    kinds = [correction_matrix(left, right) for left in (False, True) for right in (False, True)]
    mixing = edge_synthesis_matrix()
    spread = np.zeros((16, 8, X))
    spread[:, :, :HALF] = mixing[:, :8, None]
    spread[:, :, HALF:] = mixing[:, 8:, None]
    shapes = (array(*own_rebuilt.shape), array(nz, ROWS, X))
    spaces = [pltpu.VMEM] * 4 + [pltpu.SMEM] + [pltpu.VMEM] * 2
    scratch = [
        pltpu.VMEM(own_rebuilt.shape, jnp.float32),
        pltpu.SemaphoreType.DMA((nz // 4,)),
    ]
    kernel = functools.partial(halo_kernel, blocks)
    out_space = (pl.ANY, pltpu.VMEM)
    return call(kernel, shapes, spaces, scratch, "depth_halo", out_space)(
        own_rebuilt, from_right, from_left, edges, gains,
        jnp.asarray(np.stack(kinds), jnp.float32), jnp.asarray(spread.reshape(16, 8 * X), jnp.float32),
    )


def finish_kernel(own, added, coefficients):
    nz = own.shape[0]
    low = lax.broadcasted_iota(jnp.int32, (ROWS, X), 1) < HALF
    row = lax.broadcasted_iota(jnp.int32, (ROWS, X), 0)
    middle = jnp.zeros((X - 16, X), jnp.float32)
    for k in range(nz // 2):
        both = jnp.where(low, added[2 * k], pltpu.roll(added[2 * k + 1], HALF, 1))
        ends = [jnp.where(row < 4, both, 0.0), middle, jnp.where(row < 4, 0.0, both)]
        turned = jnp.concatenate(ends, 0).T
        coefficients[2 * k] = own[2 * k] + turned[:HALF]
        coefficients[2 * k + 1] = own[2 * k + 1] + turned[HALF:]


def finish(own, added):
    size = own.size
    cost = pl.CostEstimate(flops=10 * size, bytes_accessed=8 * size, transcendentals=0)
    return call(
        finish_kernel, array(*own.shape), [pltpu.VMEM] * 2, name="coefficients_halo", cost=cost
    )(own, added)


def per_device(blocks, field, gains):
    nz = lax.axis_size("aa")
    ny = field.shape[1]
    by_lines = analyse_columns(field.reshape(ny, X))
    by_depth = lax.all_to_all(by_lines.reshape(nz, ny // nz, X), "aa", 0, 0, tiled=True)
    to_left, to_right, edges = edges_of(by_depth.reshape(ny, X))
    from_right = lax.ppermute(to_left, "ba", [(k, k - 1) for k in range(1, blocks)])
    from_left = lax.ppermute(to_right, "ba", [(k, k + 1) for k in range(blocks - 1)])
    own_coefficients, own_rebuilt = main_depths(by_depth, gains, edges)
    rebuilt, added = add_halo(blocks, own_rebuilt, from_right, from_left, edges, gains)
    coefficients = finish(own_coefficients, added)
    rebuilt = lax.all_to_all(rebuilt, "aa", 0, 0, tiled=True)
    rebuilt = synthesise_columns(rebuilt.reshape(ny, X))
    return coefficients, rebuilt.reshape(1, ny, X)


def solution(mesh):
    return jax.shard_map(
        functools.partial(per_device, mesh.shape["ba"]),
        mesh=mesh,
        in_specs=(P("aa", None, "ba"), P()),
        out_specs=(P(None, "aa", "ba"), P("aa", None, "ba")),
        check_vma=False,
    )
```

time: 267 us -> 90.4 us (0.34)
  the two profiles are of different devices: /device:TPU:184 before, /device:TPU:1 now
where the time goes in v2:
time: 90.4 us; the launch traced here: 90.1 us
  blocking collectives  37.5 us (41%)
  waiting for transfers between devices  26.6 us (29%)
  starting transfers between devices  13.7 us (15%)
  Pallas kernels  11.5 us (13%)
    all_to_all x1, blocking collectives, per_device(): lax.all_to_all(by_lines.reshape(nz, ny // nz, X), 'aa', 0, 0, tiled=True)  37.5 us
    all_to_all x1, waiting for transfers between devices, per_device(): rebuilt = lax.all_to_all(rebuilt, 'aa', 0, 0, tiled=True)  26.6 us
    ppermute x1, starting transfers between devices, per_device(): lax.ppermute(to_right, 'ba', [(k, k + 1) for k in range(blocks - 1)])  7.9 us
    pallas_call x1, Pallas kernels, main_depths(): call(main_kernel, (shape, shape), spaces, name='depth_main', cost=cost)  4.66 us
    all_to_all x1, starting transfers between devices, per_device(): rebuilt = lax.all_to_all(rebuilt, 'aa', 0, 0, tiled=True)  4.48 us
    pallas_call x1, Pallas kernels, add_halo(): call(kernel, shapes, spaces, scratch, 'depth_halo', out_space)  2.25 us
  transfers between devices with their start and end apart: 3, of which 1 were waited for; matrix products, arithmetic and copies ran while one was open for 0% of the time, Pallas kernels for 7%

profile of v2, /device:TPU:1, one launch (start us, length us, event | category | flops | bytes accessed | tf_op | source)
XLA Modules:
  0.0 90.1 jit_solution(4758019928853478616)
XLA Ops:
  0.6 1.6 %analyse_y.1 = f32[2048,128]{1,0:T(8,128)S(1)} custom-call(f32[2048,128]{1,0:T(8,128)} %bitcast.8), custom_call_target="tpu_custom_call" | custom-call | tf_op jit(solution)/shard_map/analyse_y/pallas_call | solution.py:212
  2.2 37.5 %all_to_all.10.values = f32[32,64,128]{2,1,0:T(8,128)S(1)} all-to-all(f32[32,64,128]{2,1,0:T(8,128)S(1)} %bitcast.7), channel_id=1, replica_groups=mesh['aa'=32,'ba'=16] {'aa'}, dimensions={0} | all-to-all | bytes 2097152 | tf_op jit(solution)/shard_map/all_to_all | solution.py:457
  39.7 0.0 copy-start
  39.7 0.0 copy-start.1
  39.7 0.3 edges_x.1
  40.1 0.0 copy-start.4
  40.1 1.3 %collective-permute-start = (f32[4,2048]{1,0:T(4,128)S(1)}, f32[4,2048]{1,0:T(4,128)S(1)}, u32[]{:S(2)}, u32[]{:S(2)}) collective-permute-start(f32[4,2048]{1,0:T(4,128)S(1)} %get-tuple-element.12), channel_id=1, source_target_pairs={{1,0},{2,1},{3,2},{4,3},{5,4},{6,5},{7,6},{8,7},{9,8},{10,9},{11,1... | collective-permute-start | bytes 98312 | tf_op jit(solution)/shard_map/ppermute | solution.py:459
  41.4 7.9 %collective-permute-start.1 = (f32[4,2048]{1,0:T(4,128)S(1)}, f32[4,2048]{1,0:T(4,128)S(1)}, u32[]{:S(2)}, u32[]{:S(2)}) collective-permute-start(f32[4,2048]{1,0:T(4,128)S(1)} %get-tuple-element.13), channel_id=1, source_target_pairs={{0,1},{1,2},{2,3},{3,4},{4,5},{5,6},{6,7},{7,8},{8,9},{9,10},{10,1... | collective-permute-start | bytes 98312 | tf_op jit(solution)/shard_map/ppermute | solution.py:460
  49.3 0.0 copy-done
  49.3 0.0 copy-done.1
  49.3 0.0 copy-done.4
  49.3 0.0 copy-start.2
  49.3 0.0 copy-start.3
  49.4 4.7 %depth_main.1 = (f32[32,64,128]{2,1,0:T(8,128)S(1)}, f32[32,64,128]{2,1,0:T(8,128)S(1)}) custom-call(f32[32,64,128]{2,1,0:T(8,128)S(1)} %all_to_all.10.values, f32[2,2,2]{2,1,0:T(2,128)S(1)} %copy-done.4, f32[16,2048]{1,0:T(8,128)S(1)} %get-tuple-element.9.edges, f32[128,128]{1,0:T(8,128)S(1)} %copy-done.1, f32[128,128]{1,0:T(8,128)S(1)} %copy-done), custom_call_target="tpu_custom_call" | custom-call | flops 26214400 | bytes 3145728 | tf_op jit(solution)/shard_map/depth_main/pallas_call | solution.py:357
  54.0 0.0 collective-permute-done.from_right
  54.0 0.0 collective-permute-done.1.from_left
  54.0 0.0 copy-done.2
  54.1 0.0 copy-done.3
  54.1 2.2 %depth_halo.1 = (f32[32,64,128]{2,1,0:T(8,128)}, f32[32,8,128]{2,1,0:T(8,128)S(1)}) custom-call(f32[32,64,128]{2,1,0:T(8,128)S(1)} %get-tuple-element.11.own_rebuilt, f32[4,2048]{1,0:T(4,128)S(1)} %collective-permute-done.from_right, f32[4,2048]{1,0:T(4,128)S(1)} %collective-permute-done.1.from_left, f32[16,2048]{1,0:T(8,128)S(1)} %get-tuple-element.9.edges, ...), custom_call_target="tpu_custom_call" | custom-call | tf_op jit(solution)/shard_map/depth_halo/pallas_call | solution.py:426
  56.3 4.5 %all-to-all-start.1 = ((f32[32,64,128]{2,1,0:T(8,128)}), f32[32,64,128]{2,1,0:T(8,128)S(1)}, u32[]{:S(2)}, u32[]{:S(2)}) async-start(f32[32,64,128]{2,1,0:T(8,128)} %get-tuple-element.15), calls=%async_computation.1 | async-start | bytes 2097152 | tf_op jit(solution)/shard_map/all_to_all | solution.py:464
  60.8 1.4 %coefficients_halo.1 = f32[32,64,128]{2,1,0:T(8,128)} custom-call(f32[32,64,128]{2,1,0:T(8,128)S(1)} %get-tuple-element.10.own, f32[32,8,128]{2,1,0:T(8,128)S(1)} %get-tuple-element.14.added), custom_call_target="tpu_custom_call" | custom-call | flops 2621440 | bytes 2097152 | tf_op jit(solution)/shard_map/coefficients_halo/pallas_call | solution.py:448
  62.2 26.6 %all-to-all-done.1 = f32[32,64,128]{2,1,0:T(8,128)S(1)} async-done(((f32[32,64,128]{2,1,0:T(8,128)}), f32[32,64,128]{2,1,0:T(8,128)S(1)}, u32[]{:S(2)}, u32[]{:S(2)}) %all-to-all-start.1) | async-done | bytes 1048608 | tf_op jit(solution)/shard_map/all_to_all | solution.py:464
  88.8 1.3 %synthesise_y.1 = f32[2048,128]{1,0:T(8,128)} custom-call(f32[2048,128]{1,0:T(8,128)S(1)} %bitcast.6), custom_call_target="tpu_custom_call" | custom-call | tf_op jit(solution)/shard_map/synthesise_y/pallas_call | solution.py:240
Async XLA Ops:
  39.7 9.6 %copy-start = (f32[128,128]{1,0:T(8,128)S(1)}, f32[128,128]{1,0:T(8,128)}, u32[]{:S(2)}) copy-start(f32[128,128]{1,0:T(8,128)} %constant.9.clone.backward) | copy-start | bytes 196612
  39.7 9.6 %copy-start.1 = (f32[128,128]{1,0:T(8,128)S(1)}, f32[128,128]{1,0:T(8,128)}, u32[]{:S(2)}) copy-start(f32[128,128]{1,0:T(8,128)} %constant.8.clone.forward) | copy-start | bytes 196612
  40.1 9.2 %copy-start.4 = (f32[2,2,2]{2,1,0:T(2,128)S(1)}, f32[2,2,2]{2,1,0:T(2,128)}, u32[]{:S(2)}) copy-start(f32[2,2,2]{2,1,0:T(2,128)} %gains.3) | copy-start | bytes 100
  40.1 13.9 %collective-permute-start = (f32[4,2048]{1,0:T(4,128)S(1)}, f32[4,2048]{1,0:T(4,128)S(1)}, u32[]{:S(2)}, u32[]{:S(2)}) collective-permute-start(f32[4,2048]{1,0:T(4,128)S(1)} %get-tuple-element.12), channel_id=1, source_target_pairs={{1,0},{2,1},{3,2},{4,3},{5,4},{6,5},{7,6},{8,7},{9,8},{10,9},{11,1... | collective-permute-start | bytes 98312 | tf_op jit(solution)/shard_map/ppermute | solution.py:459
  41.4 12.6 %collective-permute-start.1 = (f32[4,2048]{1,0:T(4,128)S(1)}, f32[4,2048]{1,0:T(4,128)S(1)}, u32[]{:S(2)}, u32[]{:S(2)}) collective-permute-start(f32[4,2048]{1,0:T(4,128)S(1)} %get-tuple-element.13), channel_id=1, source_target_pairs={{0,1},{1,2},{2,3},{3,4},{4,5},{5,6},{6,7},{7,8},{8,9},{9,10},{10,1... | collective-permute-start | bytes 98312 | tf_op jit(solution)/shard_map/ppermute | solution.py:460
  49.3 4.7 %copy-start.2 = (f32[16,1024]{1,0:T(8,128)S(1)}, f32[16,1024]{1,0:T(8,128)}, u32[]{:S(2)}) copy-start(f32[16,1024]{1,0:T(8,128)} %constant.11.clone.spread) | copy-start | bytes 196612
  49.3 4.7 %copy-start.3 = (f32[4,16,24]{2,1,0:T(8,128)S(1)}, f32[4,16,24]{2,1,0:T(8,128)}, u32[]{:S(2)}) copy-start(f32[4,16,24]{2,1,0:T(8,128)} %constant.10.clone.weights) | copy-start | bytes 18436
  56.3 32.5 %all-to-all-start.1 = ((f32[32,64,128]{2,1,0:T(8,128)}), f32[32,64,128]{2,1,0:T(8,128)S(1)}, u32[]{:S(2)}, u32[]{:S(2)}) async-start(f32[32,64,128]{2,1,0:T(8,128)} %get-tuple-element.15), calls=%async_computation.1 | async-start | bytes 2097152 | tf_op jit(solution)/shard_map/all_to_all | solution.py:464

commit v3 on v2

--- a/solution.py
+++ b/solution.py
@@ -23,6 +23,30 @@
 VMEM_LIMIT = 24 * 1024 * 1024
 EDGE = 8
 HIGHEST = lax.Precision.HIGHEST
+
+def exchange_order(n):
+    if n != 32:
+        return [(k + 2) % n for k in range(n)]
+
+    def where(k):
+        return k // 8, k // 2 % 4, k % 2
+
+    first = 2
+
+    def distance(k):
+        (x, y, core), (x_first, y_first, core_first) = where(k), where(first)
+        along = abs(x - x_first)
+        return 10 * (min(along, 4 - along) + abs(y - y_first)) + (core != core_first)
+
+    rest = [k for k in range(n) if k != first]
+    return [first, *sorted(rest, key=lambda k: -distance(k))]
+
+
+def places(order):
+    out = [0] * len(order)
+    for k, device in enumerate(order):
+        out[device] = k
+    return out
 
 
 def edge_matrix():
@@ -149,7 +173,7 @@
     return pltpu.roll(rows, 1, 0)
 
 
-def lift_rows(line, target, at, forward):
+def lift_rows(line, target, at, forward, place):
     cells = 128
     pairs = cells // 2
     wide = pairs + 8
@@ -169,8 +193,12 @@
         d = d - C * (s + after(s))
         s = s - B * (before(d) + d)
         d = d - A * (s + after(s))
-    target[pl.ds(at, pairs, stride=2), :] = s[4 : 4 + pairs]
-    target[pl.ds(at + 1, pairs, stride=2), :] = d[4 : 4 + pairs]
+    block = target.shape[0] // len(place)
+    half = block // 2
+    for k in range(cells // block):
+        to = place[at // block + k] * block
+        target[pl.ds(to, half, stride=2), :] = s[4 + k * half : 4 + (k + 1) * half]
+        target[pl.ds(to + 1, half, stride=2), :] = d[4 + k * half : 4 + (k + 1) * half]
 
 
 def mirror_start(line):
@@ -183,7 +211,7 @@
         line[pl.ds(MARGIN + ny - 1 + k, 1), :] = line[pl.ds(MARGIN + ny - 1 - k, 1), :]
 
 
-def analyse_kernel(source, target, line, arrived):
+def analyse_kernel(order, source, target, line, arrived):
     ny = source.shape[0]
     n = ny // CHUNK
     copies = []
@@ -200,29 +228,33 @@
         else:
             mirror_end(line, ny)
         for at in range(k * CHUNK, (k + 1) * CHUNK, 128):
-            lift_rows(line, target, at, True)
-
-
-def analyse_columns(values):
+            lift_rows(line, target, at, True, places(order))
+
+
+def analyse_columns(order, values):
     ny = values.shape[0]
+    values = pltpu.with_memory_space_constraint(values, pltpu.HBM)
     scratch = [
         pltpu.VMEM((ny + 2 * MARGIN, X), jnp.float32),
         pltpu.SemaphoreType.DMA((ny // CHUNK,)),
     ]
-    return call(analyse_kernel, pltpu.VMEM((ny, X), jnp.float32), [pltpu.HBM], scratch, "analyse_y")(pltpu.with_memory_space_constraint(values, pltpu.HBM))
-
-
-def synthesise_kernel(source, target, line, lifted, left):
+    out_shape = pltpu.VMEM((ny, X), jnp.float32)
+    kernel = functools.partial(analyse_kernel, order)
+    return call(kernel, out_shape, [pltpu.HBM], scratch, "analyse_y")(values)
+
+
+def synthesise_kernel(order, source, target, line, lifted, left):
     ny = source.shape[0]
     n = ny // CHUNK
-    for k in range(n):
-        line[pl.ds(MARGIN + k * CHUNK, CHUNK), :] = source[pl.ds(k * CHUNK, CHUNK), :]
+    block = ny // len(order)
+    for k, device in enumerate(order):
+        line[pl.ds(MARGIN + device * block, block), :] = source[pl.ds(k * block, block), :]
     mirror_start(line)
     mirror_end(line, ny)
     copies = []
     for k in range(n):
         for at in range(k * CHUNK, (k + 1) * CHUNK, 128):
-            lift_rows(line, lifted, at, False)
+            lift_rows(line, lifted, at, False, range(len(order)))
         rows = pl.ds(k * CHUNK, CHUNK)
         copies.append(pltpu.make_async_copy(lifted.at[rows], target.at[rows], left.at[k]))
         copies[k].start()
@@ -230,16 +262,15 @@
         copy.wait()
 
 
-def synthesise_columns(values):
+def synthesise_columns(order, values):
     ny = values.shape[0]
     scratch = [
         pltpu.VMEM((ny + 2 * MARGIN, X), jnp.float32),
         pltpu.VMEM((ny, X), jnp.float32),
         pltpu.SemaphoreType.DMA((ny // CHUNK,)),
     ]
-    return call(
-        synthesise_kernel, array(ny, X), [pltpu.VMEM], scratch, "synthesise_y", pltpu.HBM
-    )(values)
+    kernel = functools.partial(synthesise_kernel, order)
+    return call(kernel, array(ny, X), [pltpu.VMEM], scratch, "synthesise_y", pltpu.HBM)(values)
 
 
 def edge_kernel(values, to_left, to_right, edges):
@@ -323,9 +354,10 @@
     return jnp.dot(left, right, precision=lax.Precision.HIGHEST, preferred_element_type=jnp.float32)
 
 
-def main_kernel(values, gains, edges, forward, backward, coefficients, rebuilt):
+def main_kernel(order, values, gains, edges, forward, backward, coefficients, rebuilt):
     del edges
     nz, ny, _ = values.shape
+    place = places(order)
     lane = lax.broadcasted_iota(jnp.int32, (ROWS, X), 1)
     row = lax.broadcasted_iota(jnp.int32, (ROWS, X), 0)
     gain_low, gain_high = gain_tables(gains, row % 2 == 1, lane % 2 == 1)
@@ -334,33 +366,35 @@
 
     def body(k, carry):
         rows = pl.ds(pl.multiple_of(k * ROWS, ROWS), ROWS)
-        s, d = analyse_depth([rebuilt[z, rows, :] for z in range(nz)])
+        s, d = analyse_depth([rebuilt[place[z], rows, :] for z in range(nz)])
         for n in range(nz // 2):
             coefficients[2 * n, rows, :] = s[n] * scale_low
             coefficients[2 * n + 1, rows, :] = d[n] * scale_high
         cells = synthesise_depth([v * gain_low for v in s], [v * gain_high for v in d])
         for z in range(nz):
-            rebuilt[z, rows, :] = cells[z]
+            rebuilt[place[z], rows, :] = cells[z]
         return carry
 
     lax.fori_loop(0, ny // ROWS, body, 0)
     rebuilt[...] = dot(rebuilt[...].reshape(nz * ny, X), backward[...]).reshape(nz, ny, X)
 
 
-def main_depths(values, gains, edges):
+def main_depths(order, values, gains, edges):
     shape = array(*values.shape)
     size = values.size
     cost = pl.CostEstimate(flops=100 * size, bytes_accessed=12 * size, transcendentals=0)
     spaces = [pltpu.VMEM, pltpu.SMEM, pl.ANY, pltpu.VMEM, pltpu.VMEM]
     forward = jnp.asarray(own_analysis_matrix(), jnp.float32)
     backward = jnp.asarray(synthesis_matrix()[:, :X].T, jnp.float32)
-    return call(main_kernel, (shape, shape), spaces, name="depth_main", cost=cost)(
+    kernel = functools.partial(main_kernel, order)
+    return call(kernel, (shape, shape), spaces, name="depth_main", cost=cost)(
         values, gains, edges, forward, backward
     )
 
 
 def halo_kernel(
-    blocks, own_rebuilt, from_right, from_left, edges, gains, weights, spread, rebuilt, added, held, left
+    blocks, order, own_rebuilt, from_right, from_left, edges, gains, weights, spread,
+    rebuilt, added, held, left,
 ):
     nz = own_rebuilt.shape[0]
     index = lax.axis_index("ba")
@@ -380,7 +414,7 @@
     x_odd = (row + jnp.where(low | (row < 4), 0, 1)) % 2 == 1
     gain_low, gain_high = gain_tables(gains, lane % 2 == 1, x_odd)
     scale_low, scale_high = scale_tables(x_odd)
-    s, d = analyse_depth(cells)
+    s, d = analyse_depth([cells[k] for k in places(order)])
     for n in range(nz // 2):
         added[2 * n] = s[n] * scale_low
         added[2 * n + 1] = d[n] * scale_high
@@ -390,7 +424,7 @@
     middle = jnp.zeros((X - 16, X), jnp.float32)
     for k in range(nz // 2):
         mixed = []
-        for v in cells[2 * k : 2 * k + 2]:
+        for v in (cells[order[2 * k]], cells[order[2 * k + 1]]):
             total = None
             for m in range(8):
                 term = table[m] * jnp.broadcast_to(v[m : m + 1], (16, X))
@@ -408,7 +442,7 @@
         copy.wait()
 
 
-def add_halo(blocks, own_rebuilt, from_right, from_left, edges, gains):
+def add_halo(blocks, order, own_rebuilt, from_right, from_left, edges, gains):
     nz = own_rebuilt.shape[0]
     kinds = [correction_matrix(left, right) for left in (False, True) for right in (False, True)]
     mixing = edge_synthesis_matrix()
@@ -421,7 +455,7 @@
         pltpu.VMEM(own_rebuilt.shape, jnp.float32),
         pltpu.SemaphoreType.DMA((nz // 4,)),
     ]
-    kernel = functools.partial(halo_kernel, blocks)
+    kernel = functools.partial(halo_kernel, blocks, order)
     out_space = (pl.ANY, pltpu.VMEM)
     return call(kernel, shapes, spaces, scratch, "depth_halo", out_space)(
         own_rebuilt, from_right, from_left, edges, gains,
@@ -453,16 +487,20 @@
 def per_device(blocks, field, gains):
     nz = lax.axis_size("aa")
     ny = field.shape[1]
-    by_lines = analyse_columns(field.reshape(ny, X))
-    by_depth = lax.all_to_all(by_lines.reshape(nz, ny // nz, X), "aa", 0, 0, tiled=True)
+    order = exchange_order(nz)
+
+    def exchange(blocks_):
+        blocks_ = blocks_.reshape(nz, ny // nz, X)
+        return lax.all_to_all(blocks_, "aa", 0, 0, axis_index_groups=[order], tiled=True)
+
+    by_depth = exchange(analyse_columns(order, field.reshape(ny, X)))
     to_left, to_right, edges = edges_of(by_depth.reshape(ny, X))
     from_right = lax.ppermute(to_left, "ba", [(k, k - 1) for k in range(1, blocks)])
     from_left = lax.ppermute(to_right, "ba", [(k, k + 1) for k in range(blocks - 1)])
-    own_coefficients, own_rebuilt = main_depths(by_depth, gains, edges)
-    rebuilt, added = add_halo(blocks, own_rebuilt, from_right, from_left, edges, gains)
+    own_coefficients, own_rebuilt = main_depths(order, by_depth, gains, edges)
+    rebuilt, added = add_halo(blocks, order, own_rebuilt, from_right, from_left, edges, gains)
     coefficients = finish(own_coefficients, added)
-    rebuilt = lax.all_to_all(rebuilt, "aa", 0, 0, tiled=True)
-    rebuilt = synthesise_columns(rebuilt.reshape(ny, X))
+    rebuilt = synthesise_columns(order, exchange(rebuilt).reshape(ny, X))
     return coefficients, rebuilt.reshape(1, ny, X)
 
 

time: 90.4 us -> 87.4 us (0.967)
  the two profiles are of different devices: /device:TPU:1 before, /device:TPU:256 now
where the time goes in v3:
time: 87.4 us; the launch traced here: 87.1 us
  blocking collectives  33.4 us (38%)
  waiting for transfers between devices  26.2 us (30%)
  starting transfers between devices  15.1 us (17%)
  Pallas kernels  11.6 us (13%)
    all_to_all x1, blocking collectives, exchange(): lax.all_to_all(blocks_, 'aa', 0, 0, axis_index_groups=[order], tiled=True)  33.4 us
    all_to_all x1, waiting for transfers between devices, exchange(): lax.all_to_all(blocks_, 'aa', 0, 0, axis_index_groups=[order], tiled=True)  24.1 us
    all_to_all x1, starting transfers between devices, exchange(): lax.all_to_all(blocks_, 'aa', 0, 0, axis_index_groups=[order], tiled=True)  5.31 us
    ppermute x1, starting transfers between devices, per_device(): lax.ppermute(to_right, 'ba', [(k, k + 1) for k in range(blocks - 1)])  5.07 us
    ppermute x1, starting transfers between devices, per_device(): lax.ppermute(to_left, 'ba', [(k, k - 1) for k in range(1, blocks)])  4.68 us
    pallas_call x1, Pallas kernels, main_depths(): call(kernel, (shape, shape), spaces, name='depth_main', cost=cost)  4.66 us
    pallas_call x1, Pallas kernels, add_halo(): call(kernel, shapes, spaces, scratch, 'depth_halo', out_space)  2.33 us
    ppermute x1, waiting for transfers between devices, per_device(): lax.ppermute(to_right, 'ba', [(k, k + 1) for k in range(blocks - 1)])  2.12 us
  transfers between devices with their start and end apart: 3, of which 2 were waited for; matrix products, arithmetic and copies ran while one was open for 0% of the time, Pallas kernels for 7%

profile of v3, /device:TPU:256, one launch (start us, length us, event | category | flops | bytes accessed | tf_op | source)
XLA Modules:
  0.0 87.1 jit_solution(13979539023550684885)
XLA Ops:
  0.6 1.6 %analyse_y.1 = f32[2048,128]{1,0:T(8,128)S(1)} custom-call(f32[2048,128]{1,0:T(8,128)} %bitcast.8), custom_call_target="tpu_custom_call" | custom-call | tf_op jit(solution)/shard_map/analyse_y/pallas_call | solution.py:243
  2.2 33.4 %all_to_all.10.values = f32[32,64,128]{2,1,0:T(8,128)S(1)} all-to-all(f32[32,64,128]{2,1,0:T(8,128)S(1)} %bitcast.7), channel_id=1, replica_groups={{32,368,352,240,272,336,496,224,256,320,480,112,144,208,304,400,464,96,..., dimensions={0} | all-to-all | bytes 2097152 | tf_op jit(solution)/shard_map/all_to_all | solution.py:494
  35.6 0.0 copy-start
  35.6 0.0 copy-start.1
  35.6 0.3 edges_x.1
  36.0 0.0 copy-start.4
  36.0 4.7 %collective-permute-start = (f32[4,2048]{1,0:T(4,128)S(1)}, f32[4,2048]{1,0:T(4,128)S(1)}, u32[]{:S(2)}, u32[]{:S(2)}) collective-permute-start(f32[4,2048]{1,0:T(4,128)S(1)} %get-tuple-element.12), channel_id=1, source_target_pairs={{1,0},{2,1},{3,2},{4,3},{5,4},{6,5},{7,6},{8,7},{9,8},{10,9},{11,1... | collective-permute-start | bytes 98312 | tf_op jit(solution)/shard_map/ppermute | solution.py:498
  40.7 5.1 %collective-permute-start.1 = (f32[4,2048]{1,0:T(4,128)S(1)}, f32[4,2048]{1,0:T(4,128)S(1)}, u32[]{:S(2)}, u32[]{:S(2)}) collective-permute-start(f32[4,2048]{1,0:T(4,128)S(1)} %get-tuple-element.13), channel_id=1, source_target_pairs={{0,1},{1,2},{2,3},{3,4},{4,5},{5,6},{6,7},{7,8},{8,9},{9,10},{10,1... | collective-permute-start | bytes 98312 | tf_op jit(solution)/shard_map/ppermute | solution.py:499
  45.8 0.0 copy-done
  45.8 0.0 copy-done.1
  45.8 0.0 copy-done.4
  45.8 0.0 copy-start.2
  45.8 0.0 copy-start.3
  45.8 4.7 %depth_main.1 = (f32[32,64,128]{2,1,0:T(8,128)S(1)}, f32[32,64,128]{2,1,0:T(8,128)S(1)}) custom-call(f32[32,64,128]{2,1,0:T(8,128)S(1)} %all_to_all.10.values, f32[2,2,2]{2,1,0:T(2,128)S(1)} %copy-done.4, f32[16,2048]{1,0:T(8,128)S(1)} %get-tuple-element.9.edges, f32[128,128]{1,0:T(8,128)S(1)} %copy-done.1, f32[128,128]{1,0:T(8,128)S(1)} %copy-done), custom_call_target="tpu_custom_call" | custom-call | flops 26214400 | bytes 3145728 | tf_op jit(solution)/shard_map/depth_main/pallas_call | solution.py:390
  50.5 0.0 collective-permute-done.from_right
  50.5 2.1 %collective-permute-done.1.from_left = f32[4,2048]{1,0:T(4,128)S(1)} collective-permute-done((f32[4,2048]{1,0:T(4,128)S(1)}, f32[4,2048]{1,0:T(4,128)S(1)}, u32[]{:S(2)}, u32[]{:S(2)}) %collective-permute-start.1) | collective-permute-done | bytes 32800 | tf_op jit(solution)/shard_map/ppermute | solution.py:499
  52.6 0.0 copy-done.2
  52.6 0.0 copy-done.3
  52.6 2.3 %depth_halo.1 = (f32[32,64,128]{2,1,0:T(8,128)}, f32[32,8,128]{2,1,0:T(8,128)S(1)}) custom-call(f32[32,64,128]{2,1,0:T(8,128)S(1)} %get-tuple-element.11.own_rebuilt, f32[4,2048]{1,0:T(4,128)S(1)} %collective-permute-done.from_right, f32[4,2048]{1,0:T(4,128)S(1)} %collective-permute-done.1.from_left, f32[16,2048]{1,0:T(8,128)S(1)} %get-tuple-element.9.edges, ...), custom_call_target="tpu_custom_call" | custom-call | tf_op jit(solution)/shard_map/depth_halo/pallas_call | solution.py:460
  54.9 5.3 %all-to-all-start.1 = ((f32[32,64,128]{2,1,0:T(8,128)}), f32[32,64,128]{2,1,0:T(8,128)S(1)}, u32[]{:S(2)}, u32[]{:S(2)}) async-start(f32[32,64,128]{2,1,0:T(8,128)} %get-tuple-element.15), calls=%async_computation.1 | async-start | bytes 2097152 | tf_op jit(solution)/shard_map/all_to_all | solution.py:494
  60.3 1.4 %coefficients_halo.1 = f32[32,64,128]{2,1,0:T(8,128)} custom-call(f32[32,64,128]{2,1,0:T(8,128)S(1)} %get-tuple-element.10.own, f32[32,8,128]{2,1,0:T(8,128)S(1)} %get-tuple-element.14.added), custom_call_target="tpu_custom_call" | custom-call | flops 2621440 | bytes 2097152 | tf_op jit(solution)/shard_map/coefficients_halo/pallas_call | solution.py:482
  61.6 24.1 %all-to-all-done.1 = f32[32,64,128]{2,1,0:T(8,128)S(1)} async-done(((f32[32,64,128]{2,1,0:T(8,128)}), f32[32,64,128]{2,1,0:T(8,128)S(1)}, u32[]{:S(2)}, u32[]{:S(2)}) %all-to-all-start.1) | async-done | bytes 1048608 | tf_op jit(solution)/shard_map/all_to_all | solution.py:494
  85.7 1.3 %synthesise_y.1 = f32[2048,128]{1,0:T(8,128)} custom-call(f32[2048,128]{1,0:T(8,128)S(1)} %bitcast.6), custom_call_target="tpu_custom_call" | custom-call | tf_op jit(solution)/shard_map/synthesise_y/pallas_call | solution.py:273
Async XLA Ops:
  35.6 10.1 %copy-start = (f32[128,128]{1,0:T(8,128)S(1)}, f32[128,128]{1,0:T(8,128)}, u32[]{:S(2)}) copy-start(f32[128,128]{1,0:T(8,128)} %constant.9.clone.backward) | copy-start | bytes 196612
  35.6 10.1 %copy-start.1 = (f32[128,128]{1,0:T(8,128)S(1)}, f32[128,128]{1,0:T(8,128)}, u32[]{:S(2)}) copy-start(f32[128,128]{1,0:T(8,128)} %constant.8.clone.forward) | copy-start | bytes 196612
  36.0 9.8 %copy-start.4 = (f32[2,2,2]{2,1,0:T(2,128)S(1)}, f32[2,2,2]{2,1,0:T(2,128)}, u32[]{:S(2)}) copy-start(f32[2,2,2]{2,1,0:T(2,128)} %gains.3) | copy-start | bytes 100
  36.0 14.5 %collective-permute-start = (f32[4,2048]{1,0:T(4,128)S(1)}, f32[4,2048]{1,0:T(4,128)S(1)}, u32[]{:S(2)}, u32[]{:S(2)}) collective-permute-start(f32[4,2048]{1,0:T(4,128)S(1)} %get-tuple-element.12), channel_id=1, source_target_pairs={{1,0},{2,1},{3,2},{4,3},{5,4},{6,5},{7,6},{8,7},{9,8},{10,9},{11,1... | collective-permute-start | bytes 98312 | tf_op jit(solution)/shard_map/ppermute | solution.py:498
  40.7 11.9 %collective-permute-start.1 = (f32[4,2048]{1,0:T(4,128)S(1)}, f32[4,2048]{1,0:T(4,128)S(1)}, u32[]{:S(2)}, u32[]{:S(2)}) collective-permute-start(f32[4,2048]{1,0:T(4,128)S(1)} %get-tuple-element.13), channel_id=1, source_target_pairs={{0,1},{1,2},{2,3},{3,4},{4,5},{5,6},{6,7},{7,8},{8,9},{9,10},{10,1... | collective-permute-start | bytes 98312 | tf_op jit(solution)/shard_map/ppermute | solution.py:499
  45.8 6.8 %copy-start.2 = (f32[16,1024]{1,0:T(8,128)S(1)}, f32[16,1024]{1,0:T(8,128)}, u32[]{:S(2)}) copy-start(f32[16,1024]{1,0:T(8,128)} %constant.11.clone.spread) | copy-start | bytes 196612
  45.8 6.8 %copy-start.3 = (f32[4,16,24]{2,1,0:T(8,128)S(1)}, f32[4,16,24]{2,1,0:T(8,128)}, u32[]{:S(2)}) copy-start(f32[4,16,24]{2,1,0:T(8,128)} %constant.10.clone.weights) | copy-start | bytes 18436
  54.9 30.8 %all-to-all-start.1 = ((f32[32,64,128]{2,1,0:T(8,128)}), f32[32,64,128]{2,1,0:T(8,128)S(1)}, u32[]{:S(2)}, u32[]{:S(2)}) async-start(f32[32,64,128]{2,1,0:T(8,128)} %get-tuple-element.15), calls=%async_computation.1 | async-start | bytes 2097152 | tf_op jit(solution)/shard_map/all_to_all | solution.py:494

commit v4 on v3

--- a/solution.py
+++ b/solution.py
@@ -354,7 +354,34 @@
     return jnp.dot(left, right, precision=lax.Precision.HIGHEST, preferred_element_type=jnp.float32)
 
 
-def main_kernel(order, values, gains, edges, forward, backward, coefficients, rebuilt):
+def split(values):
+    first = values.astype(jnp.bfloat16)
+    rest = values - first.astype(jnp.float32)
+    second = rest.astype(jnp.bfloat16)
+    third = (rest - second.astype(jnp.float32)).astype(jnp.bfloat16)
+    return first, second, third
+
+
+def split_matrix(matrix):
+    matrix = np.asarray(matrix, np.float32)
+    first = matrix.astype(jnp.bfloat16)
+    rest = matrix - first.astype(np.float32)
+    second = rest.astype(jnp.bfloat16)
+    third = (rest - second.astype(np.float32)).astype(jnp.bfloat16)
+    wide = np.concatenate([np.concatenate([first, second], 1)] * 2, 0)
+    return jnp.asarray(wide), jnp.asarray(np.concatenate([third, first], 0))
+
+
+def split_dot(values, wide, tall):
+    first, second, third = split(values)
+    large = jnp.dot(jnp.concatenate([first, second], 1), wide, preferred_element_type=jnp.float32)
+    small = jnp.dot(jnp.concatenate([first, third], 1), tall, preferred_element_type=jnp.float32)
+    return large[:, :X] + (large[:, X:] + small)
+
+
+def main_kernel(
+    order, values, gains, edges, forward, forward_tall, backward, backward_tall, coefficients, rebuilt
+):
     del edges
     nz, ny, _ = values.shape
     place = places(order)
@@ -362,7 +389,8 @@
     row = lax.broadcasted_iota(jnp.int32, (ROWS, X), 0)
     gain_low, gain_high = gain_tables(gains, row % 2 == 1, lane % 2 == 1)
     scale_low, scale_high = scale_tables(lane % 2 == 1)
-    rebuilt[...] = dot(values[...].reshape(nz * ny, X), forward[...]).reshape(nz, ny, X)
+    lines = split_dot(values[...].reshape(nz * ny, X), forward[...], forward_tall[...])
+    rebuilt[...] = lines.reshape(nz, ny, X)
 
     def body(k, carry):
         rows = pl.ds(pl.multiple_of(k * ROWS, ROWS), ROWS)
@@ -376,25 +404,26 @@
         return carry
 
     lax.fori_loop(0, ny // ROWS, body, 0)
-    rebuilt[...] = dot(rebuilt[...].reshape(nz * ny, X), backward[...]).reshape(nz, ny, X)
+    lines = split_dot(rebuilt[...].reshape(nz * ny, X), backward[...], backward_tall[...])
+    rebuilt[...] = lines.reshape(nz, ny, X)
 
 
 def main_depths(order, values, gains, edges):
     shape = array(*values.shape)
     size = values.size
     cost = pl.CostEstimate(flops=100 * size, bytes_accessed=12 * size, transcendentals=0)
-    spaces = [pltpu.VMEM, pltpu.SMEM, pl.ANY, pltpu.VMEM, pltpu.VMEM]
-    forward = jnp.asarray(own_analysis_matrix(), jnp.float32)
-    backward = jnp.asarray(synthesis_matrix()[:, :X].T, jnp.float32)
+    spaces = [pltpu.VMEM, pltpu.SMEM, pl.ANY] + [pltpu.VMEM] * 4
+    forward = split_matrix(own_analysis_matrix())
+    backward = split_matrix(synthesis_matrix()[:, :X].T)
     kernel = functools.partial(main_kernel, order)
     return call(kernel, (shape, shape), spaces, name="depth_main", cost=cost)(
-        values, gains, edges, forward, backward
+        values, gains, edges, *forward, *backward
     )
 
 
 def halo_kernel(
-    blocks, order, own_rebuilt, from_right, from_left, edges, gains, weights, spread,
-    rebuilt, added, held, left,
+    blocks, order, own_coefficients, own_rebuilt, from_right, from_left, edges, gains, weights, spread,
+    coefficients, rebuilt, held, left,
 ):
     nz = own_rebuilt.shape[0]
     index = lax.axis_index("ba")
@@ -415,13 +444,20 @@
     gain_low, gain_high = gain_tables(gains, lane % 2 == 1, x_odd)
     scale_low, scale_high = scale_tables(x_odd)
     s, d = analyse_depth([cells[k] for k in places(order)])
-    for n in range(nz // 2):
-        added[2 * n] = s[n] * scale_low
-        added[2 * n + 1] = d[n] * scale_high
+    middle = jnp.zeros((X - 16, X), jnp.float32)
     copies = []
+    for k in range(nz // 2):
+        both = jnp.where(low, s[k] * scale_low, pltpu.roll(d[k] * scale_high, HALF, 1))
+        ends = [jnp.where(row < 4, both, 0.0), middle, jnp.where(row < 4, 0.0, both)]
+        turned = jnp.concatenate(ends, 0).T
+        held[2 * k] = own_coefficients[2 * k] + turned[:HALF]
+        held[2 * k + 1] = own_coefficients[2 * k + 1] + turned[HALF:]
+        if k % 2 == 1:
+            part = pl.ds(2 * k - 2, 4)
+            copies.append(pltpu.make_async_copy(held.at[part], coefficients.at[part], left.at[k // 2]))
+            copies[-1].start()
     cells = synthesise_depth([v * gain_low for v in s], [v * gain_high for v in d])
     table = [spread[:, k * X : (k + 1) * X] for k in range(8)]
-    middle = jnp.zeros((X - 16, X), jnp.float32)
     for k in range(nz // 2):
         mixed = []
         for v in (cells[order[2 * k]], cells[order[2 * k + 1]]):
@@ -432,56 +468,28 @@
             mixed.append(total + pltpu.roll(total, HALF, 1))
         both = jnp.where(low_16, *mixed)
         turned = jnp.concatenate([both[:8], middle, both[8:]], 0).T
-        held[2 * k] = own_rebuilt[2 * k] + turned[:HALF]
-        held[2 * k + 1] = own_rebuilt[2 * k + 1] + turned[HALF:]
-        if k % 2 == 1:
-            part = pl.ds(2 * k - 2, 4)
-            copies.append(pltpu.make_async_copy(held.at[part], rebuilt.at[part], left.at[k // 2]))
-            copies[-1].start()
+        rebuilt[2 * k] = own_rebuilt[2 * k] + turned[:HALF]
+        rebuilt[2 * k + 1] = own_rebuilt[2 * k + 1] + turned[HALF:]
     for copy in copies:
         copy.wait()
 
 
-def add_halo(blocks, order, own_rebuilt, from_right, from_left, edges, gains):
-    nz = own_rebuilt.shape[0]
+def add_halo(blocks, order, own_coefficients, own_rebuilt, from_right, from_left, edges, gains):
+    shape = own_rebuilt.shape
+    nz = shape[0]
     kinds = [correction_matrix(left, right) for left in (False, True) for right in (False, True)]
     mixing = edge_synthesis_matrix()
     spread = np.zeros((16, 8, X))
     spread[:, :, :HALF] = mixing[:, :8, None]
     spread[:, :, HALF:] = mixing[:, 8:, None]
-    shapes = (array(*own_rebuilt.shape), array(nz, ROWS, X))
-    spaces = [pltpu.VMEM] * 4 + [pltpu.SMEM] + [pltpu.VMEM] * 2
-    scratch = [
-        pltpu.VMEM(own_rebuilt.shape, jnp.float32),
-        pltpu.SemaphoreType.DMA((nz // 4,)),
-    ]
+    spaces = [pltpu.VMEM] * 5 + [pltpu.SMEM] + [pltpu.VMEM] * 2
+    scratch = [pltpu.VMEM(shape, jnp.float32), pltpu.SemaphoreType.DMA((nz // 4,))]
     kernel = functools.partial(halo_kernel, blocks, order)
-    out_space = (pl.ANY, pltpu.VMEM)
-    return call(kernel, shapes, spaces, scratch, "depth_halo", out_space)(
-        own_rebuilt, from_right, from_left, edges, gains,
+    out_space = (pltpu.HBM, pltpu.VMEM)
+    return call(kernel, (array(*shape), array(*shape)), spaces, scratch, "depth_halo", out_space)(
+        own_coefficients, own_rebuilt, from_right, from_left, edges, gains,
         jnp.asarray(np.stack(kinds), jnp.float32), jnp.asarray(spread.reshape(16, 8 * X), jnp.float32),
     )
-
-
-def finish_kernel(own, added, coefficients):
-    nz = own.shape[0]
-    low = lax.broadcasted_iota(jnp.int32, (ROWS, X), 1) < HALF
-    row = lax.broadcasted_iota(jnp.int32, (ROWS, X), 0)
-    middle = jnp.zeros((X - 16, X), jnp.float32)
-    for k in range(nz // 2):
-        both = jnp.where(low, added[2 * k], pltpu.roll(added[2 * k + 1], HALF, 1))
-        ends = [jnp.where(row < 4, both, 0.0), middle, jnp.where(row < 4, 0.0, both)]
-        turned = jnp.concatenate(ends, 0).T
-        coefficients[2 * k] = own[2 * k] + turned[:HALF]
-        coefficients[2 * k + 1] = own[2 * k + 1] + turned[HALF:]
-
-
-def finish(own, added):
-    size = own.size
-    cost = pl.CostEstimate(flops=10 * size, bytes_accessed=8 * size, transcendentals=0)
-    return call(
-        finish_kernel, array(*own.shape), [pltpu.VMEM] * 2, name="coefficients_halo", cost=cost
-    )(own, added)
 
 
 def per_device(blocks, field, gains):
@@ -498,8 +506,9 @@
     from_right = lax.ppermute(to_left, "ba", [(k, k - 1) for k in range(1, blocks)])
     from_left = lax.ppermute(to_right, "ba", [(k, k + 1) for k in range(blocks - 1)])
     own_coefficients, own_rebuilt = main_depths(order, by_depth, gains, edges)
-    rebuilt, added = add_halo(blocks, order, own_rebuilt, from_right, from_left, edges, gains)
-    coefficients = finish(own_coefficients, added)
+    coefficients, rebuilt = add_halo(
+        blocks, order, own_coefficients, own_rebuilt, from_right, from_left, edges, gains
+    )
     rebuilt = synthesise_columns(order, exchange(rebuilt).reshape(ny, X))
     return coefficients, rebuilt.reshape(1, ny, X)
 

time: 87.4 us -> 87 us (level)
  blocking collectives: 33.4 us -> 64 us
  waiting for transfers between devices: 26.2 us -> 4.2 us
  starting transfers between devices: 15.1 us -> 9.75 us
  Pallas kernels: 11.6 us -> 8.11 us
    all_to_all x1 -> x2, blocking collectives: 33.4 us -> 64 us  [exchange(): lax.all_to_all(blocks_, 'aa', 0, 0, axis_index_groups=[order], tiled=True)]
    all_to_all x1 -> x0, waiting for transfers between devices: 24.1 us -> none  [exchange(): lax.all_to_all(blocks_, 'aa', 0, 0, axis_index_groups=[order], tiled=True)]
    all_to_all x1 -> x0, starting transfers between devices: 5.31 us -> none  [exchange(): lax.all_to_all(blocks_, 'aa', 0, 0, axis_index_groups=[order], tiled=True)]
    pallas_call x1, Pallas kernels: 4.66 us -> 2.56 us  [main_depths(): call(kernel, (shape, shape), spaces, name='depth_main', cost=cost)]
    ppermute x1, waiting for transfers between devices: 2.12 us -> 4.19 us  [per_device(): lax.ppermute(to_right, 'ba', [(k, k + 1) for k in range(blocks - 1)])]
    pallas_call x2 -> x1, Pallas kernels: 3.7 us -> 2.29 us  [add_halo(): call(kernel, (array(*shape), array(*shape)), spaces, scratch, 'depth_halo...]
  transfers between devices with their start and end apart: 3 -> 2, of which waited for: 2 -> 1; matrix products, arithmetic and copies ran while one was open for 0% -> 0% of each run, Pallas kernels for 7% -> 3%
where the time goes in v4:
time: 87 us; the launch traced here: 86.8 us
  blocking collectives  64 us (74%)
  starting transfers between devices  9.75 us (11%)
  Pallas kernels  8.11 us (9%)
  waiting for transfers between devices  4.2 us (5%)
    all_to_all x2, blocking collectives, exchange(): lax.all_to_all(blocks_, 'aa', 0, 0, axis_index_groups=[order], tiled=True)  64 us
    ppermute x1, starting transfers between devices, per_device(): lax.ppermute(to_right, 'ba', [(k, k + 1) for k in range(blocks - 1)])  5.07 us
    ppermute x1, starting transfers between devices, per_device(): lax.ppermute(to_left, 'ba', [(k, k - 1) for k in range(1, blocks)])  4.68 us
    ppermute x1, waiting for transfers between devices, per_device(): lax.ppermute(to_right, 'ba', [(k, k + 1) for k in range(blocks - 1)])  4.19 us
    pallas_call x1, Pallas kernels, main_depths(): call(kernel, (shape, shape), spaces, name='depth_main', cost=cost)  2.56 us
    pallas_call x1, Pallas kernels, add_halo(): call(kernel, (array(*shape), array(*shape)), spaces, scratch, 'depth_halo...  2.29 us
  transfers between devices with their start and end apart: 2, of which 1 were waited for; matrix products, arithmetic and copies ran while one was open for 0% of the time, Pallas kernels for 3%

profile of v4, /device:TPU:256, one launch (start us, length us, event | category | flops | bytes accessed | tf_op | source)
XLA Modules:
  0.0 86.8 jit_solution(4333470501388490754)
XLA Ops:
  0.6 1.6 %analyse_y.1 = f32[2048,128]{1,0:T(8,128)S(1)} custom-call(f32[2048,128]{1,0:T(8,128)} %bitcast.8), custom_call_target="tpu_custom_call" | custom-call | tf_op jit(solution)/shard_map/analyse_y/pallas_call | solution.py:243
  2.2 33.4 %all_to_all.10.values = f32[32,64,128]{2,1,0:T(8,128)S(1)} all-to-all(f32[32,64,128]{2,1,0:T(8,128)S(1)} %bitcast.7), channel_id=1, replica_groups={{32,368,352,240,272,336,496,224,256,320,480,112,144,208,304,400,464,96,..., dimensions={0} | all-to-all | bytes 2097152 | tf_op jit(solution)/shard_map/all_to_all | solution.py:502
  35.6 0.0 copy-start
  35.6 0.0 copy-start.1
  35.6 0.0 copy-start.3
  35.6 0.0 copy-start.4
  35.6 0.3 edges_x.1
  36.0 0.0 copy-start.6
  36.0 4.7 %collective-permute-start = (f32[4,2048]{1,0:T(4,128)S(1)}, f32[4,2048]{1,0:T(4,128)S(1)}, u32[]{:S(2)}, u32[]{:S(2)}) collective-permute-start(f32[4,2048]{1,0:T(4,128)S(1)} %get-tuple-element.12), channel_id=1, source_target_pairs={{1,0},{2,1},{3,2},{4,3},{5,4},{6,5},{7,6},{8,7},{9,8},{10,9},{11,1... | collective-permute-start | bytes 98312 | tf_op jit(solution)/shard_map/ppermute | solution.py:506
  40.7 5.1 %collective-permute-start.1 = (f32[4,2048]{1,0:T(4,128)S(1)}, f32[4,2048]{1,0:T(4,128)S(1)}, u32[]{:S(2)}, u32[]{:S(2)}) collective-permute-start(f32[4,2048]{1,0:T(4,128)S(1)} %get-tuple-element.13), channel_id=1, source_target_pairs={{0,1},{1,2},{2,3},{3,4},{4,5},{5,6},{6,7},{7,8},{8,9},{9,10},{10,1... | collective-permute-start | bytes 98312 | tf_op jit(solution)/shard_map/ppermute | solution.py:507
  45.8 0.0 copy-done
  45.8 0.0 copy-done.1
  45.8 0.0 copy-done.3
  45.8 0.0 copy-done.4
  45.8 0.0 copy-done.6
  45.8 0.0 copy-start.2
  45.8 0.0 copy-start.5
  45.8 2.6 %depth_main.1 = (f32[32,64,128]{2,1,0:T(8,128)S(1)}, f32[32,64,128]{2,1,0:T(8,128)S(1)}) custom-call(f32[32,64,128]{2,1,0:T(8,128)S(1)} %all_to_all.10.values, f32[2,2,2]{2,1,0:T(2,128)S(1)} %copy-done.6, f32[16,2048]{1,0:T(8,128)S(1)} %get-tuple-element.9.edges, bf16[256,256]{1,0:T(8,128)(2,1)S(1)} %copy-done.1, bf16[256,128]{1,0:T(8,128)(2,1)S(1)} %copy-done.4, ...), custom_call_target="tpu_custom_call" | custom-call | flops 26214400 | bytes 3145728 | tf_op jit(solution)/shard_map/depth_main/pallas_call | solution.py:419
  48.4 0.0 collective-permute-done.from_right
  48.4 4.2 %collective-permute-done.1.from_left = f32[4,2048]{1,0:T(4,128)S(1)} collective-permute-done((f32[4,2048]{1,0:T(4,128)S(1)}, f32[4,2048]{1,0:T(4,128)S(1)}, u32[]{:S(2)}, u32[]{:S(2)}) %collective-permute-start.1) | collective-permute-done | bytes 32800 | tf_op jit(solution)/shard_map/ppermute | solution.py:507
  52.6 0.0 copy-done.2
  52.6 0.0 copy-done.5
  52.6 2.3 %depth_halo.1 = (f32[32,64,128]{2,1,0:T(8,128)}, f32[32,64,128]{2,1,0:T(8,128)S(1)}) custom-call(f32[32,64,128]{2,1,0:T(8,128)S(1)} %get-tuple-element.10.own_coefficients, f32[32,64,128]{2,1,0:T(8,128)S(1)} %get-tuple-element.11.own_rebuilt, f32[4,2048]{1,0:T(4,128)S(1)} %collective-permute-done.from_right, f32[4,2048]{1,0:T(4,128)S(1)} %collective-permute-done.1.from_left, ...), custom_call_target="tpu_custom_call" | custom-call | tf_op jit(solution)/shard_map/depth_halo/pallas_call | solution.py:489
  54.9 30.6 %all_to_all.11 = f32[32,64,128]{2,1,0:T(8,128)S(1)} all-to-all(f32[32,64,128]{2,1,0:T(8,128)S(1)} %get-tuple-element.15), channel_id=1, replica_groups={{32,368,352,240,272,336,496,224,256,320,480,112,144,208,304,400,464,96,..., dimensions={0} | all-to-all | bytes 2097152 | tf_op jit(solution)/shard_map/all_to_all | solution.py:502
  85.5 1.3 %synthesise_y.1 = f32[2048,128]{1,0:T(8,128)} custom-call(f32[2048,128]{1,0:T(8,128)S(1)} %bitcast.6), custom_call_target="tpu_custom_call" | custom-call | tf_op jit(solution)/shard_map/synthesise_y/pallas_call | solution.py:273
Async XLA Ops:
  35.6 10.1 %copy-start = (bf16[256,256]{1,0:T(8,128)(2,1)S(1)}, bf16[256,256]{1,0:T(8,128)(2,1)}, u32[]{:S(2)}) copy-start(bf16[256,256]{1,0:T(8,128)(2,1)} %constant.14.clone.backward) | copy-start | bytes 393220
  35.6 10.2 %copy-start.1 = (bf16[256,256]{1,0:T(8,128)(2,1)S(1)}, bf16[256,256]{1,0:T(8,128)(2,1)}, u32[]{:S(2)}) copy-start(bf16[256,256]{1,0:T(8,128)(2,1)} %constant.12.clone.forward) | copy-start | bytes 393220
  35.6 10.2 %copy-start.3 = (bf16[256,128]{1,0:T(8,128)(2,1)S(1)}, bf16[256,128]{1,0:T(8,128)(2,1)}, u32[]{:S(2)}) copy-start(bf16[256,128]{1,0:T(8,128)(2,1)} %constant.15.clone.backward_tall) | copy-start | bytes 196612
  35.6 10.2 %copy-start.4 = (bf16[256,128]{1,0:T(8,128)(2,1)S(1)}, bf16[256,128]{1,0:T(8,128)(2,1)}, u32[]{:S(2)}) copy-start(bf16[256,128]{1,0:T(8,128)(2,1)} %constant.13.clone.forward_tall) | copy-start | bytes 196612
  36.0 9.8 %copy-start.6 = (f32[2,2,2]{2,1,0:T(2,128)S(1)}, f32[2,2,2]{2,1,0:T(2,128)}, u32[]{:S(2)}) copy-start(f32[2,2,2]{2,1,0:T(2,128)} %gains.3) | copy-start | bytes 100
  36.0 12.4 %collective-permute-start = (f32[4,2048]{1,0:T(4,128)S(1)}, f32[4,2048]{1,0:T(4,128)S(1)}, u32[]{:S(2)}, u32[]{:S(2)}) collective-permute-start(f32[4,2048]{1,0:T(4,128)S(1)} %get-tuple-element.12), channel_id=1, source_target_pairs={{1,0},{2,1},{3,2},{4,3},{5,4},{6,5},{7,6},{8,7},{9,8},{10,9},{11,1... | collective-permute-start | bytes 98312 | tf_op jit(solution)/shard_map/ppermute | solution.py:506
  40.7 11.9 %collective-permute-start.1 = (f32[4,2048]{1,0:T(4,128)S(1)}, f32[4,2048]{1,0:T(4,128)S(1)}, u32[]{:S(2)}, u32[]{:S(2)}) collective-permute-start(f32[4,2048]{1,0:T(4,128)S(1)} %get-tuple-element.13), channel_id=1, source_target_pairs={{0,1},{1,2},{2,3},{3,4},{4,5},{5,6},{6,7},{7,8},{8,9},{9,10},{10,1... | collective-permute-start | bytes 98312 | tf_op jit(solution)/shard_map/ppermute | solution.py:507
  45.8 6.8 %copy-start.2 = (f32[16,1024]{1,0:T(8,128)S(1)}, f32[16,1024]{1,0:T(8,128)}, u32[]{:S(2)}) copy-start(f32[16,1024]{1,0:T(8,128)} %constant.17.clone.spread) | copy-start | bytes 196612
  45.8 6.8 %copy-start.5 = (f32[4,16,24]{2,1,0:T(8,128)S(1)}, f32[4,16,24]{2,1,0:T(8,128)}, u32[]{:S(2)}) copy-start(f32[4,16,24]{2,1,0:T(8,128)} %constant.16.clone.weights) | copy-start | bytes 18436

commit v5 on v4

--- a/solution.py
+++ b/solution.py
@@ -31,7 +31,7 @@
     def where(k):
         return k // 8, k // 2 % 4, k % 2
 
-    first = 2
+    first = 11
 
     def distance(k):
         (x, y, core), (x_first, y_first, core_first) = where(k), where(first)

time: 87 us -> 85.6 us (0.984)
  the two profiles are of different devices: /device:TPU:256 before, /device:TPU:265 now
where the time goes in v5:
time: 85.6 us; the launch traced here: 85.4 us
  blocking collectives  63.7 us (74%)
  starting transfers between devices  9.19 us (11%)
  Pallas kernels  8.11 us (9%)
  waiting for transfers between devices  3.56 us (4%)
    all_to_all x2, blocking collectives, exchange(): lax.all_to_all(blocks_, 'aa', 0, 0, axis_index_groups=[order], tiled=True)  63.7 us
    ppermute x1, starting transfers between devices, per_device(): lax.ppermute(to_right, 'ba', [(k, k + 1) for k in range(blocks - 1)])  4.79 us
    ppermute x1, starting transfers between devices, per_device(): lax.ppermute(to_left, 'ba', [(k, k - 1) for k in range(1, blocks)])  4.4 us
    ppermute x1, waiting for transfers between devices, per_device(): lax.ppermute(to_right, 'ba', [(k, k + 1) for k in range(blocks - 1)])  3.56 us
    pallas_call x1, Pallas kernels, main_depths(): call(kernel, (shape, shape), spaces, name='depth_main', cost=cost)  2.57 us
    pallas_call x1, Pallas kernels, add_halo(): call(kernel, (array(*shape), array(*shape)), spaces, scratch, 'depth_halo...  2.29 us
  transfers between devices with their start and end apart: 2, of which 1 were waited for; matrix products, arithmetic and copies ran while one was open for 0% of the time, Pallas kernels for 3%

profile of v5, /device:TPU:265, one launch (start us, length us, event | category | flops | bytes accessed | tf_op | source)
XLA Modules:
  0.0 85.4 jit_solution(95583421505535357)
XLA Ops:
  0.6 1.6 %analyse_y.1 = f32[2048,128]{1,0:T(8,128)S(1)} custom-call(f32[2048,128]{1,0:T(8,128)} %bitcast.8), custom_call_target="tpu_custom_call" | custom-call | tf_op jit(solution)/shard_map/analyse_y/pallas_call | solution.py:243
  2.2 33.1 %all_to_all.10.values = f32[32,64,128]{2,1,0:T(8,128)S(1)} all-to-all(f32[32,64,128]{2,1,0:T(8,128)S(1)} %bitcast.7), channel_id=1, replica_groups={{176,480,496,96,352,384,448,112,368,400,464,0,64,224,256,320,416,16,80,..., dimensions={0} | all-to-all | bytes 2097152 | tf_op jit(solution)/shard_map/all_to_all | solution.py:502
  35.3 0.0 copy-start
  35.3 0.0 copy-start.1
  35.3 0.0 copy-start.3
  35.3 0.0 copy-start.4
  35.3 0.3 edges_x.1
  35.6 0.0 copy-start.6
  35.7 4.4 %collective-permute-start = (f32[4,2048]{1,0:T(4,128)S(1)}, f32[4,2048]{1,0:T(4,128)S(1)}, u32[]{:S(2)}, u32[]{:S(2)}) collective-permute-start(f32[4,2048]{1,0:T(4,128)S(1)} %get-tuple-element.12), channel_id=1, source_target_pairs={{1,0},{2,1},{3,2},{4,3},{5,4},{6,5},{7,6},{8,7},{9,8},{10,9},{11,1... | collective-permute-start | bytes 98312 | tf_op jit(solution)/shard_map/ppermute | solution.py:506
  40.1 4.8 %collective-permute-start.1 = (f32[4,2048]{1,0:T(4,128)S(1)}, f32[4,2048]{1,0:T(4,128)S(1)}, u32[]{:S(2)}, u32[]{:S(2)}) collective-permute-start(f32[4,2048]{1,0:T(4,128)S(1)} %get-tuple-element.13), channel_id=1, source_target_pairs={{0,1},{1,2},{2,3},{3,4},{4,5},{5,6},{6,7},{7,8},{8,9},{9,10},{10,1... | collective-permute-start | bytes 98312 | tf_op jit(solution)/shard_map/ppermute | solution.py:507
  44.9 0.0 copy-done
  44.9 0.0 copy-done.1
  44.9 0.0 copy-done.3
  44.9 0.0 copy-done.4
  44.9 0.0 copy-done.6
  44.9 0.0 copy-start.2
  44.9 0.0 copy-start.5
  44.9 2.6 %depth_main.1 = (f32[32,64,128]{2,1,0:T(8,128)S(1)}, f32[32,64,128]{2,1,0:T(8,128)S(1)}) custom-call(f32[32,64,128]{2,1,0:T(8,128)S(1)} %all_to_all.10.values, f32[2,2,2]{2,1,0:T(2,128)S(1)} %copy-done.6, f32[16,2048]{1,0:T(8,128)S(1)} %get-tuple-element.9.edges, bf16[256,256]{1,0:T(8,128)(2,1)S(1)} %copy-done.1, bf16[256,128]{1,0:T(8,128)(2,1)S(1)} %copy-done.4, ...), custom_call_target="tpu_custom_call" | custom-call | flops 26214400 | bytes 3145728 | tf_op jit(solution)/shard_map/depth_main/pallas_call | solution.py:419
  47.5 0.0 collective-permute-done.from_right
  47.5 3.6 %collective-permute-done.1.from_left = f32[4,2048]{1,0:T(4,128)S(1)} collective-permute-done((f32[4,2048]{1,0:T(4,128)S(1)}, f32[4,2048]{1,0:T(4,128)S(1)}, u32[]{:S(2)}, u32[]{:S(2)}) %collective-permute-start.1) | collective-permute-done | bytes 32800 | tf_op jit(solution)/shard_map/ppermute | solution.py:507
  51.1 0.0 copy-done.2
  51.1 0.0 copy-done.5
  51.1 2.3 %depth_halo.1 = (f32[32,64,128]{2,1,0:T(8,128)}, f32[32,64,128]{2,1,0:T(8,128)S(1)}) custom-call(f32[32,64,128]{2,1,0:T(8,128)S(1)} %get-tuple-element.10.own_coefficients, f32[32,64,128]{2,1,0:T(8,128)S(1)} %get-tuple-element.11.own_rebuilt, f32[4,2048]{1,0:T(4,128)S(1)} %collective-permute-done.from_right, f32[4,2048]{1,0:T(4,128)S(1)} %collective-permute-done.1.from_left, ...), custom_call_target="tpu_custom_call" | custom-call | tf_op jit(solution)/shard_map/depth_halo/pallas_call | solution.py:489
  53.4 30.7 %all_to_all.11 = f32[32,64,128]{2,1,0:T(8,128)S(1)} all-to-all(f32[32,64,128]{2,1,0:T(8,128)S(1)} %get-tuple-element.15), channel_id=1, replica_groups={{176,480,496,96,352,384,448,112,368,400,464,0,64,224,256,320,416,16,80,..., dimensions={0} | all-to-all | bytes 2097152 | tf_op jit(solution)/shard_map/all_to_all | solution.py:502
  84.0 1.3 %synthesise_y.1 = f32[2048,128]{1,0:T(8,128)} custom-call(f32[2048,128]{1,0:T(8,128)S(1)} %bitcast.6), custom_call_target="tpu_custom_call" | custom-call | tf_op jit(solution)/shard_map/synthesise_y/pallas_call | solution.py:273
Async XLA Ops:
  35.3 9.6 %copy-start = (bf16[256,256]{1,0:T(8,128)(2,1)S(1)}, bf16[256,256]{1,0:T(8,128)(2,1)}, u32[]{:S(2)}) copy-start(bf16[256,256]{1,0:T(8,128)(2,1)} %constant.14.clone.backward) | copy-start | bytes 393220
  35.3 9.6 %copy-start.1 = (bf16[256,256]{1,0:T(8,128)(2,1)S(1)}, bf16[256,256]{1,0:T(8,128)(2,1)}, u32[]{:S(2)}) copy-start(bf16[256,256]{1,0:T(8,128)(2,1)} %constant.12.clone.forward) | copy-start | bytes 393220
  35.3 9.6 %copy-start.3 = (bf16[256,128]{1,0:T(8,128)(2,1)S(1)}, bf16[256,128]{1,0:T(8,128)(2,1)}, u32[]{:S(2)}) copy-start(bf16[256,128]{1,0:T(8,128)(2,1)} %constant.15.clone.backward_tall) | copy-start | bytes 196612
  35.3 9.6 %copy-start.4 = (bf16[256,128]{1,0:T(8,128)(2,1)S(1)}, bf16[256,128]{1,0:T(8,128)(2,1)}, u32[]{:S(2)}) copy-start(bf16[256,128]{1,0:T(8,128)(2,1)} %constant.13.clone.forward_tall) | copy-start | bytes 196612
  35.6 9.3 %copy-start.6 = (f32[2,2,2]{2,1,0:T(2,128)S(1)}, f32[2,2,2]{2,1,0:T(2,128)}, u32[]{:S(2)}) copy-start(f32[2,2,2]{2,1,0:T(2,128)} %gains.3) | copy-start | bytes 100
  35.7 11.9 %collective-permute-start = (f32[4,2048]{1,0:T(4,128)S(1)}, f32[4,2048]{1,0:T(4,128)S(1)}, u32[]{:S(2)}, u32[]{:S(2)}) collective-permute-start(f32[4,2048]{1,0:T(4,128)S(1)} %get-tuple-element.12), channel_id=1, source_target_pairs={{1,0},{2,1},{3,2},{4,3},{5,4},{6,5},{7,6},{8,7},{9,8},{10,9},{11,1... | collective-permute-start | bytes 98312 | tf_op jit(solution)/shard_map/ppermute | solution.py:506
  40.1 11.0 %collective-permute-start.1 = (f32[4,2048]{1,0:T(4,128)S(1)}, f32[4,2048]{1,0:T(4,128)S(1)}, u32[]{:S(2)}, u32[]{:S(2)}) collective-permute-start(f32[4,2048]{1,0:T(4,128)S(1)} %get-tuple-element.13), channel_id=1, source_target_pairs={{0,1},{1,2},{2,3},{3,4},{4,5},{5,6},{6,7},{7,8},{8,9},{9,10},{10,1... | collective-permute-start | bytes 98312 | tf_op jit(solution)/shard_map/ppermute | solution.py:507
  44.9 6.2 %copy-start.2 = (f32[16,1024]{1,0:T(8,128)S(1)}, f32[16,1024]{1,0:T(8,128)}, u32[]{:S(2)}) copy-start(f32[16,1024]{1,0:T(8,128)} %constant.17.clone.spread) | copy-start | bytes 196612
  44.9 6.2 %copy-start.5 = (f32[4,16,24]{2,1,0:T(8,128)S(1)}, f32[4,16,24]{2,1,0:T(8,128)}, u32[]{:S(2)}) copy-start(f32[4,16,24]{2,1,0:T(8,128)} %constant.16.clone.weights) | copy-start | bytes 18436

commit v6 on v5

--- a/solution.py
+++ b/solution.py
@@ -379,10 +379,16 @@
     return large[:, :X] + (large[:, X:] + small)
 
 
+def end_kind(blocks):
+    index = lax.axis_index("ba")
+    return 2 * (index == 0).astype(jnp.int32) + (index == blocks - 1).astype(jnp.int32)
+
+
 def main_kernel(
-    order, values, gains, edges, forward, forward_tall, backward, backward_tall, coefficients, rebuilt
+    blocks, order, values, gains, edges, forward, forward_tall, backward, backward_tall, weights,
+    coefficients, rebuilt, own_rows,
 ):
-    del edges
+    own_rows[...] = dot(weights[end_kind(blocks)], edges[...])
     nz, ny, _ = values.shape
     place = places(order)
     lane = lax.broadcasted_iota(jnp.int32, (ROWS, X), 1)
@@ -408,36 +414,49 @@
     rebuilt[...] = lines.reshape(nz, ny, X)
 
 
-def main_depths(order, values, gains, edges):
+def correction_kinds():
+    return np.stack([correction_matrix(a, b) for a in (False, True) for b in (False, True)])
+
+
+def main_depths(blocks, order, values, gains, edges):
     shape = array(*values.shape)
     size = values.size
     cost = pl.CostEstimate(flops=100 * size, bytes_accessed=12 * size, transcendentals=0)
-    spaces = [pltpu.VMEM, pltpu.SMEM, pl.ANY] + [pltpu.VMEM] * 4
+    spaces = [pltpu.VMEM, pltpu.SMEM] + [pltpu.VMEM] * 6
+    weights = jnp.asarray(correction_kinds()[:, :, 8:], jnp.float32)
     forward = split_matrix(own_analysis_matrix())
     backward = split_matrix(synthesis_matrix()[:, :X].T)
-    kernel = functools.partial(main_kernel, order)
-    return call(kernel, (shape, shape), spaces, name="depth_main", cost=cost)(
-        values, gains, edges, *forward, *backward
+    kernel = functools.partial(main_kernel, blocks, order)
+    shapes = (shape, shape, array(*edges.shape))
+    return call(kernel, shapes, spaces, name="depth_main", cost=cost)(
+        values, gains, edges, *forward, *backward, weights
     )
 
 
 def halo_kernel(
-    blocks, order, own_coefficients, own_rebuilt, from_right, from_left, edges, gains, weights, spread,
+    blocks, order, own_coefficients, own_rebuilt, from_right, from_left, own_rows, gains, weights, spread,
     coefficients, rebuilt, held, left,
 ):
     nz = own_rebuilt.shape[0]
-    index = lax.axis_index("ba")
-    kind = 2 * (index == 0).astype(jnp.int32) + (index == blocks - 1).astype(jnp.int32)
-    halo = jnp.concatenate([from_right[...], from_left[...], edges[...]], 0)
-    found = dot(weights[kind], halo)
+    kind = end_kind(blocks)
+    weight = [weights[kind, :, k * X : (k + 1) * X] for k in range(7)]
+
+    def rows_of(at):
+        found = own_rows[:, at : at + X]
+        for k in range(7):
+            source, row = (from_right, k) if k < 4 else (from_left, k - 4)
+            halo = source[row : row + 1, at : at + X]
+            found = found + weight[k] * jnp.broadcast_to(halo, (16, X))
+        return found
+
     lane = lax.broadcasted_iota(jnp.int32, (ROWS, X), 1)
     row = lax.broadcasted_iota(jnp.int32, (ROWS, X), 0)
     low = lane < HALF
     low_16 = lax.broadcasted_iota(jnp.int32, (16, X), 1) < HALF
     cells = []
     for k in range(nz // 2):
-        inside = found[0:8, k * X : (k + 1) * X]
-        beyond = found[8:16, k * X : (k + 1) * X]
+        found = rows_of(k * X)
+        inside, beyond = found[0:8], found[8:16]
         cells.append(jnp.where(low, inside, pltpu.roll(beyond, HALF, 1)))
         cells.append(jnp.where(low, pltpu.roll(inside, HALF, 1), beyond))
     x_odd = (row + jnp.where(low | (row < 4), 0, 1)) % 2 == 1
@@ -474,10 +493,10 @@
         copy.wait()
 
 
-def add_halo(blocks, order, own_coefficients, own_rebuilt, from_right, from_left, edges, gains):
+def add_halo(blocks, order, own_coefficients, own_rebuilt, from_right, from_left, own_rows, gains):
     shape = own_rebuilt.shape
     nz = shape[0]
-    kinds = [correction_matrix(left, right) for left in (False, True) for right in (False, True)]
+    weights = np.repeat(correction_kinds()[:, :, :7], X, 2)
     mixing = edge_synthesis_matrix()
     spread = np.zeros((16, 8, X))
     spread[:, :, :HALF] = mixing[:, :8, None]
@@ -487,8 +506,8 @@
     kernel = functools.partial(halo_kernel, blocks, order)
     out_space = (pltpu.HBM, pltpu.VMEM)
     return call(kernel, (array(*shape), array(*shape)), spaces, scratch, "depth_halo", out_space)(
-        own_coefficients, own_rebuilt, from_right, from_left, edges, gains,
-        jnp.asarray(np.stack(kinds), jnp.float32), jnp.asarray(spread.reshape(16, 8 * X), jnp.float32),
+        own_coefficients, own_rebuilt, from_right, from_left, own_rows, gains,
+        jnp.asarray(weights, jnp.float32), jnp.asarray(spread.reshape(16, 8 * X), jnp.float32),
     )
 
 
@@ -505,9 +524,9 @@
     to_left, to_right, edges = edges_of(by_depth.reshape(ny, X))
     from_right = lax.ppermute(to_left, "ba", [(k, k - 1) for k in range(1, blocks)])
     from_left = lax.ppermute(to_right, "ba", [(k, k + 1) for k in range(blocks - 1)])
-    own_coefficients, own_rebuilt = main_depths(order, by_depth, gains, edges)
+    own_coefficients, own_rebuilt, own_rows = main_depths(blocks, order, by_depth, gains, edges)
     coefficients, rebuilt = add_halo(
-        blocks, order, own_coefficients, own_rebuilt, from_right, from_left, edges, gains
+        blocks, order, own_coefficients, own_rebuilt, from_right, from_left, own_rows, gains
     )
     rebuilt = synthesise_columns(order, exchange(rebuilt).reshape(ny, X))
     return coefficients, rebuilt.reshape(1, ny, X)

time: 85.6 us -> 85.4 us (level)
  no operation moved by 1% of the time
where the time goes in v6:
time: 85.4 us; the launch traced here: 85.2 us
  blocking collectives  63.7 us (75%)
  starting transfers between devices  9.19 us (11%)
  Pallas kernels  8.05 us (9%)
  waiting for transfers between devices  3.39 us (4%)
    all_to_all x2, blocking collectives, exchange(): lax.all_to_all(blocks_, 'aa', 0, 0, axis_index_groups=[order], tiled=True)  63.7 us
    ppermute x1, starting transfers between devices, per_device(): lax.ppermute(to_right, 'ba', [(k, k + 1) for k in range(blocks - 1)])  4.79 us
    ppermute x1, starting transfers between devices, per_device(): lax.ppermute(to_left, 'ba', [(k, k - 1) for k in range(1, blocks)])  4.4 us
    ppermute x1, waiting for transfers between devices, per_device(): lax.ppermute(to_right, 'ba', [(k, k + 1) for k in range(blocks - 1)])  3.39 us
    pallas_call x1, Pallas kernels, main_depths(): call(kernel, shapes, spaces, name='depth_main', cost=cost)  2.72 us
    pallas_call x1, Pallas kernels, add_halo(): call(kernel, (array(*shape), array(*shape)), spaces, scratch, 'depth_halo...  2.08 us
  transfers between devices with their start and end apart: 2, of which 1 were waited for; matrix products, arithmetic and copies ran while one was open for 0% of the time, Pallas kernels for 3%

profile of v6, /device:TPU:265, one launch (start us, length us, event | category | flops | bytes accessed | tf_op | source)
XLA Modules:
  0.0 85.2 jit_solution(7178746093278074154)
XLA Ops:
  0.6 1.6 %analyse_y.1 = f32[2048,128]{1,0:T(8,128)S(1)} custom-call(f32[2048,128]{1,0:T(8,128)} %bitcast.8), custom_call_target="tpu_custom_call" | custom-call | tf_op jit(solution)/shard_map/analyse_y/pallas_call | solution.py:243
  2.2 33.1 %all_to_all.10.values = f32[32,64,128]{2,1,0:T(8,128)S(1)} all-to-all(f32[32,64,128]{2,1,0:T(8,128)S(1)} %bitcast.7), channel_id=1, replica_groups={{176,480,496,96,352,384,448,112,368,400,464,0,64,224,256,320,416,16,80,..., dimensions={0} | all-to-all | bytes 2097152 | tf_op jit(solution)/shard_map/all_to_all | solution.py:521
  35.3 0.0 copy-start.1
  35.3 0.0 copy-start.2
  35.3 0.0 copy-start.4
  35.3 0.0 copy-start.5
  35.3 0.0 copy-start.6
  35.3 0.3 edges_x.1
  35.7 0.0 copy-start.7
  35.7 4.4 %collective-permute-start = (f32[4,2048]{1,0:T(4,128)S(1)}, f32[4,2048]{1,0:T(4,128)S(1)}, u32[]{:S(2)}, u32[]{:S(2)}) collective-permute-start(f32[4,2048]{1,0:T(4,128)S(1)} %get-tuple-element.13), channel_id=1, source_target_pairs={{1,0},{2,1},{3,2},{4,3},{5,4},{6,5},{7,6},{8,7},{9,8},{10,9},{11,1... | collective-permute-start | bytes 98312 | tf_op jit(solution)/shard_map/ppermute | solution.py:525
  40.1 4.8 %collective-permute-start.1 = (f32[4,2048]{1,0:T(4,128)S(1)}, f32[4,2048]{1,0:T(4,128)S(1)}, u32[]{:S(2)}, u32[]{:S(2)}) collective-permute-start(f32[4,2048]{1,0:T(4,128)S(1)} %get-tuple-element.14), channel_id=1, source_target_pairs={{0,1},{1,2},{2,3},{3,4},{4,5},{5,6},{6,7},{7,8},{8,9},{9,10},{10,1... | collective-permute-start | bytes 98312 | tf_op jit(solution)/shard_map/ppermute | solution.py:526
  44.9 0.0 copy-done.1
  44.9 0.0 copy-done.2
  44.9 0.0 copy-done.4
  44.9 0.0 copy-done.5
  44.9 0.0 copy-done.6
  44.9 0.0 copy-done.7
  44.9 0.0 copy-start
  44.9 0.0 copy-start.3
  45.0 2.7 %depth_main.1 = (f32[32,64,128]{2,1,0:T(8,128)S(1)}, f32[32,64,128]{2,1,0:T(8,128)S(1)}, f32[16,2048]{1,0:T(8,128)S(1)}) custom-call(f32[32,64,128]{2,1,0:T(8,128)S(1)} %all_to_all.10.values, f32[2,2,2]{2,1,0:T(2,128)S(1)} %copy-done.7, f32[16,2048]{1,0:T(8,128)S(1)} %get-tuple-element.10.edges, bf16[256,256]{1,0:T(8,128)(2,1)S(1)} %copy-done.2, ...), custom_call_target="tpu_custom_call" | custom-call | flops 26214400 | bytes 3145728 | tf_op jit(solution)/shard_map/depth_main/pallas_call | solution.py:431
  47.7 0.0 collective-permute-done.from_right
  47.7 3.4 %collective-permute-done.1.from_left = f32[4,2048]{1,0:T(4,128)S(1)} collective-permute-done((f32[4,2048]{1,0:T(4,128)S(1)}, f32[4,2048]{1,0:T(4,128)S(1)}, u32[]{:S(2)}, u32[]{:S(2)}) %collective-permute-start.1) | collective-permute-done | bytes 32800 | tf_op jit(solution)/shard_map/ppermute | solution.py:526
  51.1 0.0 copy-done
  51.1 0.0 copy-done.3
  51.1 2.1 %depth_halo.1 = (f32[32,64,128]{2,1,0:T(8,128)}, f32[32,64,128]{2,1,0:T(8,128)S(1)}) custom-call(f32[32,64,128]{2,1,0:T(8,128)S(1)} %get-tuple-element.11.own_coefficients, f32[32,64,128]{2,1,0:T(8,128)S(1)} %get-tuple-element.12.own_rebuilt, f32[4,2048]{1,0:T(4,128)S(1)} %collective-permute-done.from_right, f32[4,2048]{1,0:T(4,128)S(1)} %collective-permute-done.1.from_left, ...), custom_call_target="tpu_custom_call" | custom-call | tf_op jit(solution)/shard_map/depth_halo/pallas_call | solution.py:508
  53.2 30.7 %all_to_all.11 = f32[32,64,128]{2,1,0:T(8,128)S(1)} all-to-all(f32[32,64,128]{2,1,0:T(8,128)S(1)} %get-tuple-element.17), channel_id=1, replica_groups={{176,480,496,96,352,384,448,112,368,400,464,0,64,224,256,320,416,16,80,..., dimensions={0} | all-to-all | bytes 2097152 | tf_op jit(solution)/shard_map/all_to_all | solution.py:521
  83.8 1.3 %synthesise_y.1 = f32[2048,128]{1,0:T(8,128)} custom-call(f32[2048,128]{1,0:T(8,128)S(1)} %bitcast.6), custom_call_target="tpu_custom_call" | custom-call | tf_op jit(solution)/shard_map/synthesise_y/pallas_call | solution.py:273
Async XLA Ops:
  35.3 9.6 %copy-start.1 = (bf16[256,256]{1,0:T(8,128)(2,1)S(1)}, bf16[256,256]{1,0:T(8,128)(2,1)}, u32[]{:S(2)}) copy-start(bf16[256,256]{1,0:T(8,128)(2,1)} %constant.17.clone.backward) | copy-start | bytes 393220
  35.3 9.6 %copy-start.2 = (bf16[256,256]{1,0:T(8,128)(2,1)S(1)}, bf16[256,256]{1,0:T(8,128)(2,1)}, u32[]{:S(2)}) copy-start(bf16[256,256]{1,0:T(8,128)(2,1)} %constant.15.clone.forward) | copy-start | bytes 393220
  35.3 9.6 %copy-start.4 = (bf16[256,128]{1,0:T(8,128)(2,1)S(1)}, bf16[256,128]{1,0:T(8,128)(2,1)}, u32[]{:S(2)}) copy-start(bf16[256,128]{1,0:T(8,128)(2,1)} %constant.18.clone.backward_tall) | copy-start | bytes 196612
  35.3 9.6 %copy-start.5 = (bf16[256,128]{1,0:T(8,128)(2,1)S(1)}, bf16[256,128]{1,0:T(8,128)(2,1)}, u32[]{:S(2)}) copy-start(bf16[256,128]{1,0:T(8,128)(2,1)} %constant.16.clone.forward_tall) | copy-start | bytes 196612
  35.3 9.6 %copy-start.6 = (f32[4,16,16]{2,1,0:T(8,128)S(1)}, f32[4,16,16]{2,1,0:T(8,128)}, u32[]{:S(2)}) copy-start(f32[4,16,16]{2,1,0:T(8,128)} %constant.14.clone.weights) | copy-start | bytes 12292
  35.7 9.3 %copy-start.7 = (f32[2,2,2]{2,1,0:T(2,128)S(1)}, f32[2,2,2]{2,1,0:T(2,128)}, u32[]{:S(2)}) copy-start(f32[2,2,2]{2,1,0:T(2,128)} %gains.3) | copy-start | bytes 100
  35.7 12.0 %collective-permute-start = (f32[4,2048]{1,0:T(4,128)S(1)}, f32[4,2048]{1,0:T(4,128)S(1)}, u32[]{:S(2)}, u32[]{:S(2)}) collective-permute-start(f32[4,2048]{1,0:T(4,128)S(1)} %get-tuple-element.13), channel_id=1, source_target_pairs={{1,0},{2,1},{3,2},{4,3},{5,4},{6,5},{7,6},{8,7},{9,8},{10,9},{11,1... | collective-permute-start | bytes 98312 | tf_op jit(solution)/shard_map/ppermute | solution.py:525
  40.1 11.0 %collective-permute-start.1 = (f32[4,2048]{1,0:T(4,128)S(1)}, f32[4,2048]{1,0:T(4,128)S(1)}, u32[]{:S(2)}, u32[]{:S(2)}) collective-permute-start(f32[4,2048]{1,0:T(4,128)S(1)} %get-tuple-element.14), channel_id=1, source_target_pairs={{0,1},{1,2},{2,3},{3,4},{4,5},{5,6},{6,7},{7,8},{8,9},{9,10},{10,1... | collective-permute-start | bytes 98312 | tf_op jit(solution)/shard_map/ppermute | solution.py:526
  44.9 6.2 %copy-start = (f32[4,16,896]{2,1,0:T(8,128)S(1)}, f32[4,16,896]{2,1,0:T(8,128)}, u32[]{:S(2)}) copy-start(f32[4,16,896]{2,1,0:T(8,128)} %constant.19.clone.weights) | copy-start | bytes 688132
  44.9 6.1 %copy-start.3 = (f32[16,1024]{1,0:T(8,128)S(1)}, f32[16,1024]{1,0:T(8,128)}, u32[]{:S(2)}) copy-start(f32[16,1024]{1,0:T(8,128)} %constant.20.clone.spread) | copy-start | bytes 196612

commit v7 on v6

--- a/solution.py
+++ b/solution.py
@@ -39,7 +39,8 @@
         return 10 * (min(along, 4 - along) + abs(y - y_first)) + (core != core_first)
 
     rest = [k for k in range(n) if k != first]
-    return [first, *sorted(rest, key=lambda k: -distance(k))]
+    rest = sorted(rest, key=lambda k: -distance(k))
+    return [first, *rest[22:], *rest[:22]]
 
 
 def places(order):

time: 85.4 us -> 85.1 us (level)
  the two profiles are of different devices: /device:TPU:265 before, /device:TPU:261 now
where the time goes in v7:
time: 85.1 us; the launch traced here: 84.8 us
  blocking collectives  63.7 us (75%)
  starting transfers between devices  9.19 us (11%)
  Pallas kernels  8.07 us (9%)
  waiting for transfers between devices  3.07 us (4%)
    all_to_all x2, blocking collectives, exchange(): lax.all_to_all(blocks_, 'aa', 0, 0, axis_index_groups=[order], tiled=True)  63.7 us
    ppermute x1, starting transfers between devices, per_device(): lax.ppermute(to_right, 'ba', [(k, k + 1) for k in range(blocks - 1)])  4.79 us
    ppermute x1, starting transfers between devices, per_device(): lax.ppermute(to_left, 'ba', [(k, k - 1) for k in range(1, blocks)])  4.4 us
    ppermute x1, waiting for transfers between devices, per_device(): lax.ppermute(to_right, 'ba', [(k, k + 1) for k in range(blocks - 1)])  3.07 us
    pallas_call x1, Pallas kernels, main_depths(): call(kernel, shapes, spaces, name='depth_main', cost=cost)  2.74 us
    pallas_call x1, Pallas kernels, add_halo(): call(kernel, (array(*shape), array(*shape)), spaces, scratch, 'depth_halo...  2.08 us
  transfers between devices with their start and end apart: 2, of which 1 were waited for; matrix products, arithmetic and copies ran while one was open for 0% of the time, Pallas kernels for 3%

profile of v7, /device:TPU:261, one launch (start us, length us, event | category | flops | bytes accessed | tf_op | source)
XLA Modules:
  0.0 84.8 jit_solution(15894130544559794893)
XLA Ops:
  0.6 1.6 %analyse_y.1 = f32[2048,128]{1,0:T(8,128)S(1)} custom-call(f32[2048,128]{1,0:T(8,128)} %bitcast.8), custom_call_target="tpu_custom_call" | custom-call | tf_op jit(solution)/shard_map/analyse_y/pallas_call | solution.py:244
  2.2 32.2 %all_to_all.10.values = f32[32,64,128]{2,1,0:T(8,128)S(1)} all-to-all(f32[32,64,128]{2,1,0:T(8,128)S(1)} %bitcast.7), channel_id=1, replica_groups={{176,32,128,192,288,48,144,208,304,160,480,496,96,352,384,448,112,368,4..., dimensions={0} | all-to-all | bytes 2097152 | tf_op jit(solution)/shard_map/all_to_all | solution.py:522
  34.5 0.0 copy-start.1
  34.5 0.0 copy-start.2
  34.5 0.0 copy-start.4
  34.5 0.0 copy-start.5
  34.5 0.0 copy-start.6
  34.5 0.3 edges_x.1
  34.8 0.0 copy-start.7
  34.8 4.4 %collective-permute-start = (f32[4,2048]{1,0:T(4,128)S(1)}, f32[4,2048]{1,0:T(4,128)S(1)}, u32[]{:S(2)}, u32[]{:S(2)}) collective-permute-start(f32[4,2048]{1,0:T(4,128)S(1)} %get-tuple-element.13), channel_id=1, source_target_pairs={{1,0},{2,1},{3,2},{4,3},{5,4},{6,5},{7,6},{8,7},{9,8},{10,9},{11,1... | collective-permute-start | bytes 98312 | tf_op jit(solution)/shard_map/ppermute | solution.py:526
  39.3 4.8 %collective-permute-start.1 = (f32[4,2048]{1,0:T(4,128)S(1)}, f32[4,2048]{1,0:T(4,128)S(1)}, u32[]{:S(2)}, u32[]{:S(2)}) collective-permute-start(f32[4,2048]{1,0:T(4,128)S(1)} %get-tuple-element.14), channel_id=1, source_target_pairs={{0,1},{1,2},{2,3},{3,4},{4,5},{5,6},{6,7},{7,8},{8,9},{9,10},{10,1... | collective-permute-start | bytes 98312 | tf_op jit(solution)/shard_map/ppermute | solution.py:527
  44.1 0.0 copy-done.1
  44.1 0.0 copy-done.2
  44.1 0.0 copy-done.4
  44.1 0.0 copy-done.5
  44.1 0.0 copy-done.6
  44.1 0.0 copy-done.7
  44.1 0.0 copy-start
  44.1 0.0 copy-start.3
  44.1 2.7 %depth_main.1 = (f32[32,64,128]{2,1,0:T(8,128)S(1)}, f32[32,64,128]{2,1,0:T(8,128)S(1)}, f32[16,2048]{1,0:T(8,128)S(1)}) custom-call(f32[32,64,128]{2,1,0:T(8,128)S(1)} %all_to_all.10.values, f32[2,2,2]{2,1,0:T(2,128)S(1)} %copy-done.7, f32[16,2048]{1,0:T(8,128)S(1)} %get-tuple-element.10.edges, bf16[256,256]{1,0:T(8,128)(2,1)S(1)} %copy-done.2, ...), custom_call_target="tpu_custom_call" | custom-call | flops 26214400 | bytes 3145728 | tf_op jit(solution)/shard_map/depth_main/pallas_call | solution.py:432
  46.9 0.0 collective-permute-done.from_right
  46.9 3.1 %collective-permute-done.1.from_left = f32[4,2048]{1,0:T(4,128)S(1)} collective-permute-done((f32[4,2048]{1,0:T(4,128)S(1)}, f32[4,2048]{1,0:T(4,128)S(1)}, u32[]{:S(2)}, u32[]{:S(2)}) %collective-permute-start.1) | collective-permute-done | bytes 32800 | tf_op jit(solution)/shard_map/ppermute | solution.py:527
  50.0 0.0 copy-done
  50.0 0.0 copy-done.3
  50.0 2.1 %depth_halo.1 = (f32[32,64,128]{2,1,0:T(8,128)}, f32[32,64,128]{2,1,0:T(8,128)S(1)}) custom-call(f32[32,64,128]{2,1,0:T(8,128)S(1)} %get-tuple-element.11.own_coefficients, f32[32,64,128]{2,1,0:T(8,128)S(1)} %get-tuple-element.12.own_rebuilt, f32[4,2048]{1,0:T(4,128)S(1)} %collective-permute-done.from_right, f32[4,2048]{1,0:T(4,128)S(1)} %collective-permute-done.1.from_left, ...), custom_call_target="tpu_custom_call" | custom-call | tf_op jit(solution)/shard_map/depth_halo/pallas_call | solution.py:509
  52.1 31.5 %all_to_all.11 = f32[32,64,128]{2,1,0:T(8,128)S(1)} all-to-all(f32[32,64,128]{2,1,0:T(8,128)S(1)} %get-tuple-element.17), channel_id=1, replica_groups={{176,32,128,192,288,48,144,208,304,160,480,496,96,352,384,448,112,368,4..., dimensions={0} | all-to-all | bytes 2097152 | tf_op jit(solution)/shard_map/all_to_all | solution.py:522
  83.5 1.3 %synthesise_y.1 = f32[2048,128]{1,0:T(8,128)} custom-call(f32[2048,128]{1,0:T(8,128)S(1)} %bitcast.6), custom_call_target="tpu_custom_call" | custom-call | tf_op jit(solution)/shard_map/synthesise_y/pallas_call | solution.py:274
Async XLA Ops:
  34.5 9.6 %copy-start.1 = (bf16[256,256]{1,0:T(8,128)(2,1)S(1)}, bf16[256,256]{1,0:T(8,128)(2,1)}, u32[]{:S(2)}) copy-start(bf16[256,256]{1,0:T(8,128)(2,1)} %constant.17.clone.backward) | copy-start | bytes 393220
  34.5 9.6 %copy-start.2 = (bf16[256,256]{1,0:T(8,128)(2,1)S(1)}, bf16[256,256]{1,0:T(8,128)(2,1)}, u32[]{:S(2)}) copy-start(bf16[256,256]{1,0:T(8,128)(2,1)} %constant.15.clone.forward) | copy-start | bytes 393220
  34.5 9.6 %copy-start.4 = (bf16[256,128]{1,0:T(8,128)(2,1)S(1)}, bf16[256,128]{1,0:T(8,128)(2,1)}, u32[]{:S(2)}) copy-start(bf16[256,128]{1,0:T(8,128)(2,1)} %constant.18.clone.backward_tall) | copy-start | bytes 196612
  34.5 9.6 %copy-start.5 = (bf16[256,128]{1,0:T(8,128)(2,1)S(1)}, bf16[256,128]{1,0:T(8,128)(2,1)}, u32[]{:S(2)}) copy-start(bf16[256,128]{1,0:T(8,128)(2,1)} %constant.16.clone.forward_tall) | copy-start | bytes 196612
  34.5 9.6 %copy-start.6 = (f32[4,16,16]{2,1,0:T(8,128)S(1)}, f32[4,16,16]{2,1,0:T(8,128)}, u32[]{:S(2)}) copy-start(f32[4,16,16]{2,1,0:T(8,128)} %constant.14.clone.weights) | copy-start | bytes 12292
  34.8 9.3 %copy-start.7 = (f32[2,2,2]{2,1,0:T(2,128)S(1)}, f32[2,2,2]{2,1,0:T(2,128)}, u32[]{:S(2)}) copy-start(f32[2,2,2]{2,1,0:T(2,128)} %gains.3) | copy-start | bytes 100
  34.8 12.0 %collective-permute-start = (f32[4,2048]{1,0:T(4,128)S(1)}, f32[4,2048]{1,0:T(4,128)S(1)}, u32[]{:S(2)}, u32[]{:S(2)}) collective-permute-start(f32[4,2048]{1,0:T(4,128)S(1)} %get-tuple-element.13), channel_id=1, source_target_pairs={{1,0},{2,1},{3,2},{4,3},{5,4},{6,5},{7,6},{8,7},{9,8},{10,9},{11,1... | collective-permute-start | bytes 98312 | tf_op jit(solution)/shard_map/ppermute | solution.py:526
  39.3 10.7 %collective-permute-start.1 = (f32[4,2048]{1,0:T(4,128)S(1)}, f32[4,2048]{1,0:T(4,128)S(1)}, u32[]{:S(2)}, u32[]{:S(2)}) collective-permute-start(f32[4,2048]{1,0:T(4,128)S(1)} %get-tuple-element.14), channel_id=1, source_target_pairs={{0,1},{1,2},{2,3},{3,4},{4,5},{5,6},{6,7},{7,8},{8,9},{9,10},{10,1... | collective-permute-start | bytes 98312 | tf_op jit(solution)/shard_map/ppermute | solution.py:527
  44.1 5.9 %copy-start = (f32[4,16,896]{2,1,0:T(8,128)S(1)}, f32[4,16,896]{2,1,0:T(8,128)}, u32[]{:S(2)}) copy-start(f32[4,16,896]{2,1,0:T(8,128)} %constant.19.clone.weights) | copy-start | bytes 688132
  44.1 5.8 %copy-start.3 = (f32[16,1024]{1,0:T(8,128)S(1)}, f32[16,1024]{1,0:T(8,128)}, u32[]{:S(2)}) copy-start(f32[16,1024]{1,0:T(8,128)} %constant.20.clone.spread) | copy-start | bytes 196612
